TPU v7x, 128 devices: a whole 4x4x4 slice. The times are simulated.
128 devices in a mesh: cable: 32 (over x, y_lo, z), seg: 4 (over y_hi, core).
Axes of the slice: x: 4, y: 4 (y_hi: 2, y_lo: 2; y = y_hi * 2 + y_lo), z: 4, core: 2. Of those that a mesh axis runs over, the one named last changes fastest.
Arguments:
- frames: bfloat16 [4096, 64, 256], P('seg', 'cable'), may hold values from -6 to 6
- tension: float32 [4096, 64], P('seg', 'cable'), may hold values from 0.1 to 10
- step_index: int32 [256], replicated, may hold values from 0 to 15
- owner_map: int32 [64], replicated, may hold values from 0 to 63, each once
- old_basis: bfloat16 [4, 1024, 64, 256], P('seg', 'cable'), may hold values from -6 to 6
- singular: float32 [256], replicated, may hold values from 0.5 to 5
Outputs:
- factor: float32 [512, 512], replicated
- new_basis: bfloat16 [4, 1024, 64, 512], P('seg', 'cable')
Inputs may be any that keep to these rules, and one draw needn't show every extreme that they name: `owner_map`: each streamer number appears exactly once.
All inputs are finite; a program needn't handle non-finite values.
Results may differ from a plain program's by a relative error of at most 0.001.
The roundings to bfloat16 on the way count: a program that leaves them out, or rounds other values in their place, can miss the bound.
Values may be sent and summed in bfloat16 or wider, within the bound.
A program may use at most 64 MiB of HBM per device.

v0:
```python
import jax
import jax.numpy as jnp
from jax import lax
from jax.sharding import PartitionSpec as P

K = 256
SNAP = 256
SWEEPS = 6


drag_rate = 0.1


def padded_2(block, sides, width):
    for axis, dim in sides:
        count = lax.axis_size(axis)
        forward = [(i, i + 1) for i in range(count - 1)]
        backward = [(target, source) for source, target in forward]
        low = lax.ppermute(
            lax.slice_in_dim(block, block.shape[dim] - width, None, axis=dim), axis, forward
        )
        high = lax.ppermute(lax.slice_in_dim(block, 0, width, axis=dim), axis, backward)
        block = jnp.concatenate([low, block, high], axis=dim)
    return block


def body(frames, tension, step_index, owner_map, old_basis, singular):
    stiffness = drag_rate * (1.0 + step_index.astype(jnp.float32))
    tension_wide = padded_2(tension, (("seg", 0),), 1)
    left_weight = (0.5 * (tension_wide[:-2] + tension_wide[1:-1]))[:, :, None]
    right_weight = (0.5 * (tension_wide[1:-1] + tension_wide[2:]))[:, :, None]
    denom = 1.0 + stiffness * (left_weight + right_weight)
    source = frames.astype(jnp.float32)
    current = source
    for repeat in range(SWEEPS):
        padded = padded_2(current, (("seg", 0),), 1)
        current = (
            source + stiffness * (right_weight * padded[2:] + left_weight * padded[:-2])
        ) / denom
    solved = current.astype(jnp.bfloat16)
    width = K + SNAP
    arrived = lax.all_to_all(solved, "cable", split_axis=0, concat_axis=1, tiled=True)
    ordered = jnp.take(arrived, owner_map, axis=1)
    scaled_basis = (old_basis[0] * singular).astype(jnp.bfloat16)
    stacked = jnp.concatenate([scaled_basis, ordered], axis=-1)
    flat_rows = stacked.reshape(-1, width)
    gram_local = lax.dot_general(
        flat_rows, flat_rows, (((0,), (0,)), ((), ())), preferred_element_type=jnp.float32
    )
    gram_sum = lax.psum(gram_local, ("cable", "seg"))
    rows_all = flat_rows.shape[0] * lax.axis_size("cable") * lax.axis_size("seg")
    gram_sum = gram_sum / rows_all
    lower_chol = jnp.linalg.cholesky(gram_sum)
    factor = jnp.transpose(lower_chol)
    identity_m = jnp.eye(width, dtype=jnp.float32)
    inverse_bf = jnp.transpose(
        jax.scipy.linalg.solve_triangular(lower_chol, identity_m, lower=True)
    ).astype(jnp.bfloat16)
    rotated = jnp.dot(flat_rows, inverse_bf, preferred_element_type=jnp.float32).astype(
        jnp.bfloat16
    )
    rotated = rotated.reshape(stacked.shape[0], stacked.shape[1], width)
    new_basis = rotated[None]
    return (factor, new_basis)


def solution(mesh):
    return jax.shard_map(
        body,
        mesh=mesh,
        in_specs=(
            P("seg", "cable", None),
            P("seg", "cable"),
            P(),
            P(),
            P("seg", "cable", None, None),
            P(),
        ),
        out_specs=(P(), P("seg", "cable", None, None)),
        check_vma=False,
    )
```

profile of v0, /device:TPU:1, one launch (start us, length us, event | category | flops | bytes accessed | tf_op | source)
XLA Modules:
  0.0 443.1 jit_solution(12020397310554846247)
XLA Ops:
  8.0 3.3 collective-permute-start
  11.3 4.8 %collective-permute-start.2 = (f32[1,2]{0,1:T(2,128)S(1)}, f32[1,2]{0,1:T(2,128)S(1)}, u32[]{:S(2)}, u32[]{:S(2)}) collective-permute-start(f32[1,2]{0,1:T(2,128)S(1)} %get-tuple-element.55), channel_id=1, source_target_pairs={{0,1},{1,2},{2,3},{4,5},{5,6},{6,7},{8,9},{9,10},{10,11},{12,13},{... | collective-permute-start | bytes 32 | tf_op jit(solution)/shard_map/ppermute | solution.py:19
  18.8 5.3 %collective-permute-start.3 = (f32[1,2,256]{2,1,0:T(2,128)S(1)}, f32[1,2,256]{2,1,0:T(2,128)S(1)}, u32[]{:S(2)}, u32[]{:S(2)}) collective-permute-start(f32[1,2,256]{2,1,0:T(2,128)S(1)} %get-tuple-element.44), channel_id=1, source_target_pairs={{0,1},{1,2},{2,3},{4,5},{5,6},{6,7},{8,9},{9,10},{10,11},{12,13},{... | collective-permute-start | bytes 6152 | tf_op jit(solution)/shard_map/ppermute | solution.py:19
  24.0 3.3 convert_element_type.42
  28.2 7.6 %fusion = f32[1024,2,256]{2,1,0:T(2,128)S(1)} fusion(bf16[1024,2,256]{2,1,0:T(2,128)(2,1)S(1)} %copy-done, f32[1024,2,256]{2,1,0:T(2,128)} %convert_element_type.42, f32[1,2,256]{2,1,0:T(2,128)S(1)} %collective-permute-done.3, f32[1,2,256]{2,1,0:T(2,128)S(1)} %collective-permute-done.1, f32[1024,2]{1,0:T(8,128)S(1)} %copy.29, f32[1024,2]{1,0:T(8,128)S(1)} %copy.28, ...), kind=kLoop, calls=%fused_computation.10 | loop fusion | flops 5767168 | bytes 5272576 | tf_op jit(solution)/shard_map/div | solution.py:37
  37.7 5.1 %collective-permute-start.5 = (f32[1,2,256]{2,1,0:T(2,128)S(1)}, f32[1,2,256]{2,1,0:T(2,128)S(1)}, u32[]{:S(2)}, u32[]{:S(2)}) collective-permute-start(f32[1,2,256]{2,1,0:T(2,128)S(1)} %get-tuple-element.40), channel_id=1, source_target_pairs={{0,1},{1,2},{2,3},{4,5},{5,6},{6,7},{8,9},{9,10},{10,11},{12,13},{... | collective-permute-start | bytes 6152 | tf_op jit(solution)/shard_map/ppermute | solution.py:19
  43.6 6.3 %fusion.1 = f32[1024,2,256]{2,1,0:T(2,128)S(1)} fusion(bf16[1024,2,256]{2,1,0:T(2,128)(2,1)S(1)} %copy-done, f32[1024,2,256]{2,1,0:T(2,128)S(1)} %fusion, f32[1,2,256]{2,1,0:T(2,128)S(1)} %collective-permute-done.5, f32[1,2,256]{2,1,0:T(2,128)S(1)} %collective-permute-done.4, f32[1024,2]{1,0:T(8,128)S(1)} %copy.29, f32[1024,2]{1,0:T(8,128)S(1)} %copy.28, ...), kind=kLoop, calls=%fused_computation.11 | loop fusion | flops 5767168 | bytes 5272576 | tf_op jit(solution)/shard_map/div | solution.py:37
  51.8 5.7 %collective-permute-start.7 = (f32[1,2,256]{2,1,0:T(2,128)S(1)}, f32[1,2,256]{2,1,0:T(2,128)S(1)}, u32[]{:S(2)}, u32[]{:S(2)}) collective-permute-start(f32[1,2,256]{2,1,0:T(2,128)S(1)} %get-tuple-element.38), channel_id=1, source_target_pairs={{0,1},{1,2},{2,3},{4,5},{5,6},{6,7},{8,9},{9,10},{10,11},{12,13},{... | collective-permute-start | bytes 6152 | tf_op jit(solution)/shard_map/ppermute | solution.py:19
  58.2 6.3 %fusion.2 = f32[1024,2,256]{2,1,0:T(2,128)S(1)} fusion(bf16[1024,2,256]{2,1,0:T(2,128)(2,1)S(1)} %copy-done, f32[1024,2,256]{2,1,0:T(2,128)S(1)} %fusion.1, f32[1,2,256]{2,1,0:T(2,128)S(1)} %collective-permute-done.7, f32[1,2,256]{2,1,0:T(2,128)S(1)} %collective-permute-done.6, f32[1024,2]{1,0:T(8,128)S(1)} %copy.29, f32[1024,2]{1,0:T(8,128)S(1)} %copy.28, ...), kind=kLoop, calls=%fused_computation.12 | loop fusion | flops 5767168 | bytes 5272576 | tf_op jit(solution)/shard_map/div | solution.py:37
  66.5 5.7 %collective-permute-start.9 = (f32[1,2,256]{2,1,0:T(2,128)S(1)}, f32[1,2,256]{2,1,0:T(2,128)S(1)}, u32[]{:S(2)}, u32[]{:S(2)}) collective-permute-start(f32[1,2,256]{2,1,0:T(2,128)S(1)} %get-tuple-element.36), channel_id=1, source_target_pairs={{0,1},{1,2},{2,3},{4,5},{5,6},{6,7},{8,9},{9,10},{10,11},{12,13},{... | collective-permute-start | bytes 6152 | tf_op jit(solution)/shard_map/ppermute | solution.py:19
  72.9 6.3 %fusion.3 = f32[1024,2,256]{2,1,0:T(2,128)S(1)} fusion(bf16[1024,2,256]{2,1,0:T(2,128)(2,1)S(1)} %copy-done, f32[1024,2,256]{2,1,0:T(2,128)S(1)} %fusion.2, f32[1,2,256]{2,1,0:T(2,128)S(1)} %collective-permute-done.9, f32[1,2,256]{2,1,0:T(2,128)S(1)} %collective-permute-done.8, f32[1024,2]{1,0:T(8,128)S(1)} %copy.29, f32[1024,2]{1,0:T(8,128)S(1)} %copy.28, ...), kind=kLoop, calls=%fused_computation.13 | loop fusion | flops 5767168 | bytes 5272576 | tf_op jit(solution)/shard_map/div | solution.py:37
  81.2 5.7 %collective-permute-start.11 = (f32[1,2,256]{2,1,0:T(2,128)S(1)}, f32[1,2,256]{2,1,0:T(2,128)S(1)}, u32[]{:S(2)}, u32[]{:S(2)}) collective-permute-start(f32[1,2,256]{2,1,0:T(2,128)S(1)} %get-tuple-element.34), channel_id=1, source_target_pairs={{0,1},{1,2},{2,3},{4,5},{5,6},{6,7},{8,9},{9,10},{10,11},{12,13},{... | collective-permute-start | bytes 6152 | tf_op jit(solution)/shard_map/ppermute | solution.py:19
  87.9 6.3 %fusion.4 = f32[1024,2,256]{2,1,0:T(2,128)S(1)} fusion(bf16[1024,2,256]{2,1,0:T(2,128)(2,1)S(1)} %copy-done, f32[1024,2,256]{2,1,0:T(2,128)S(1)} %fusion.3, f32[1,2,256]{2,1,0:T(2,128)S(1)} %collective-permute-done.11, f32[1,2,256]{2,1,0:T(2,128)S(1)} %collective-permute-done.10, f32[1024,2]{1,0:T(8,128)S(1)} %copy.29, f32[1024,2]{1,0:T(8,128)S(1)} %copy.28, ...), kind=kLoop, calls=%fused_computation.14 | loop fusion | flops 5767168 | bytes 5272576 | tf_op jit(solution)/shard_map/div | solution.py:37
  96.2 5.3 %collective-permute-start.13 = (f32[1,2,256]{2,1,0:T(2,128)S(1)}, f32[1,2,256]{2,1,0:T(2,128)S(1)}, u32[]{:S(2)}, u32[]{:S(2)}) collective-permute-start(f32[1,2,256]{2,1,0:T(2,128)S(1)} %get-tuple-element.32), channel_id=1, source_target_pairs={{0,1},{1,2},{2,3},{4,5},{5,6},{6,7},{8,9},{9,10},{10,11},{12,13},{... | collective-permute-start | bytes 6152 | tf_op jit(solution)/shard_map/ppermute | solution.py:19
  102.2 7.1 %fusion.39 = bf16[1024,2,256]{2,1,0:T(2,128)(2,1)} fusion(f32[1024,2,256]{2,1,0:T(2,128)S(1)} %fusion.4, f32[1,2,256]{2,1,0:T(2,128)S(1)} %collective-permute-done.13, f32[1,2,256]{2,1,0:T(2,128)S(1)} %collective-permute-done.12, bf16[1024,2,256]{2,1,0:T(2,128)(2,1)S(1)} %copy-done, f32[1024,2]{1,0:T(8,128)S(1)} %copy.29, f32[1024,2]{1,0:T(8,128)S(1)} %copy.28, ...), kind=kLoop, calls=%fused_computation.64 | loop fusion | flops 6291456 | bytes 4224000 | tf_op jit(solution)/shard_map/convert_element_type | solution.py:40
  109.3 8.8 %all-to-all-start = ((bf16[1024,2,256]{2,1,0:T(2,128)(2,1)}), bf16[1024,2,256]{2,1,0:T(2,128)(2,1)S(1)}, u32[]{:S(2)}, u32[]{:S(2)}) async-start(bf16[1024,2,256]{2,1,0:T(2,128)(2,1)} %fusion.39), calls=%async_computation | async-start | bytes 2097152 | tf_op jit(solution)/shard_map/all_to_all | solution.py:42
  119.7 13.4 %all-to-all-done = bf16[1024,2,256]{2,1,0:T(2,128)(2,1)S(1)} async-done(((bf16[1024,2,256]{2,1,0:T(2,128)(2,1)}), bf16[1024,2,256]{2,1,0:T(2,128)(2,1)S(1)}, u32[]{:S(2)}, u32[]{:S(2)}) %all-to-all-start) | async-done | bytes 1048608 | tf_op jit(solution)/shard_map/all_to_all | solution.py:42
  139.1 143.9 %all-reduce.3.cloned.1.call-done = f32[512,512]{0,1:T(8,128)} async-done(((f32[512,512]{0,1:T(8,128)}), f32[512,512]{0,1:T(8,128)}) %all-reduce.3.cloned.1.call-update) | async-done | bytes 1048592 | tf_op jit(solution)/shard_map/psum | solution.py:50
  285.0 11.7 %cholesky.104 = f32[128,128]{1,0:T(8,128)S(1)} custom-call(f32[128,128]{1,0:T(8,128)S(1)} %cholesky.266), custom_call_target="Cholesky" | custom-call | tf_op jit(solution)/shard_map/jit(cholesky)/cholesky | solution.py:53
  296.9 9.8 %custom-call.31 = f32[1,128,128]{1,2,0:T(8,128)S(1)} custom-call(f32[1,128,128]{2,1,0:T(8,128)S(1)} %get-tuple-element.54), custom_call_target="InvertDiagBlocksLowerTriangular" | custom-call | tf_op jit(solution)/shard_map/jit(cholesky)/cholesky | solution.py:53
  307.4 11.7 %cholesky.217 = f32[128,128]{1,0:T(8,128)S(1)} custom-call(f32[128,128]{1,0:T(8,128)S(1)} %cholesky.270), custom_call_target="Cholesky" | custom-call | tf_op jit(solution)/shard_map/jit(cholesky)/cholesky | solution.py:53
  319.1 10.0 %custom-call.32 = f32[1,128,128]{1,2,0:T(8,128)S(1)} custom-call(f32[1,128,128]{2,1,0:T(8,128)S(1)} %get-tuple-element.51), custom_call_target="InvertDiagBlocksLowerTriangular" | custom-call | tf_op jit(solution)/shard_map/jit(cholesky)/cholesky | solution.py:53
  329.8 11.7 %cholesky.238 = f32[128,128]{1,0:T(8,128)S(1)} custom-call(f32[128,128]{1,0:T(8,128)S(1)} %cholesky.275), custom_call_target="Cholesky" | custom-call | tf_op jit(solution)/shard_map/jit(cholesky)/cholesky | solution.py:53
  342.2 9.8 %custom-call.33 = f32[1,128,128]{1,2,0:T(8,128)S(1)} custom-call(f32[1,128,128]{2,1,0:T(8,128)S(1)} %get-tuple-element.48), custom_call_target="InvertDiagBlocksLowerTriangular" | custom-call | tf_op jit(solution)/shard_map/jit(cholesky)/cholesky | solution.py:53
  352.6 11.7 %cholesky.255 = f32[128,128]{1,0:T(8,128)S(1)} custom-call(f32[128,128]{1,0:T(8,128)S(1)} %convolution_subtract_fusion.5), custom_call_target="Cholesky" | custom-call | tf_op jit(solution)/shard_map/jit(cholesky)/cholesky | solution.py:53
  369.9 14.0 %while.1 = (s32[]{:T(128)}, f32[512,512]{1,0:T(8,128)}, s32[4,2]{0,1:T(2,128)S(1)}, f32[4,128,128]{2,1,0:T(8,128)}, s32[]{:T(128)}) while((s32[]{:T(128)}, f32[512,512]{1,0:T(8,128)}, s32[4,2]{0,1:T(2,128)S(1)}, f32[4,128,128]{2,1,0:T(8,128)}, s32[]{:T(128)}) %tuple.48), condition=%wide.while_cond, body=%wide.while_body.sunk | while | flops 2 | bytes 132705 | solution.py:57
  370.5 2.9 bitcast_dynamic-update-slice_fusion.2
  374.0 2.9 bitcast_dynamic-update-slice_fusion.2
  377.5 2.9 bitcast_dynamic-update-slice_fusion.2
  381.0 2.8 bitcast_dynamic-update-slice_fusion.2
  383.8 40.1 %custom-call.34 = f32[4,128,128]{1,2,0:T(8,128)S(1)} custom-call(f32[4,128,128]{2,1,0:T(8,128)} %get-tuple-element.9), custom_call_target="InvertDiagBlocksLowerTriangular" | custom-call | tf_op jit(solution)/shard_map/jit(_solve_triangular)/triangular_solve | solution.py:57
  432.0 3.8 convolution_convert_fusion
  (110 shorter events, 43.1 us)
Async XLA Ops:
  7.2 20.2 %copy-start.6 = (f32[1024,2]{0,1:T(2,128)S(1)}, f32[1024,2]{0,1:T(2,128)}, u32[]{:S(2)}) copy-start(f32[1024,2]{0,1:T(2,128)} %param.7) | copy-start | bytes 24580
  7.2 20.1 %copy-start.8 = (s32[256]{0:T(256)S(1)}, s32[256]{0:T(256)}, u32[]{:S(2)}) copy-start(s32[256]{0:T(256)} %param.8) | copy-start | bytes 3076
  8.0 19.3 %collective-permute-start = (f32[1,2]{0,1:T(2,128)S(1)}, f32[1,2]{0,1:T(2,128)S(1)}, u32[]{:S(2)}, u32[]{:S(2)}) collective-permute-start(f32[1,2]{0,1:T(2,128)S(1)} %get-tuple-element.56), channel_id=1, source_target_pairs={{1,0},{2,1},{3,2},{5,4},{6,5},{7,6},{9,8},{10,9},{11,10},{13,12},{... | collective-permute-start | bytes 32 | tf_op jit(solution)/shard_map/ppermute | solution.py:22
  11.3 16.0 %collective-permute-start.2 = (f32[1,2]{0,1:T(2,128)S(1)}, f32[1,2]{0,1:T(2,128)S(1)}, u32[]{:S(2)}, u32[]{:S(2)}) collective-permute-start(f32[1,2]{0,1:T(2,128)S(1)} %get-tuple-element.55), channel_id=1, source_target_pairs={{0,1},{1,2},{2,3},{4,5},{5,6},{6,7},{8,9},{9,10},{10,11},{12,13},{... | collective-permute-start | bytes 32 | tf_op jit(solution)/shard_map/ppermute | solution.py:19
  16.8 11.3 %collective-permute-start.1 = (f32[1,2,256]{2,1,0:T(2,128)S(1)}, f32[1,2,256]{2,1,0:T(2,128)S(1)}, u32[]{:S(2)}, u32[]{:S(2)}) collective-permute-start(f32[1,2,256]{2,1,0:T(2,128)S(1)} %get-tuple-element.43), channel_id=1, source_target_pairs={{1,0},{2,1},{3,2},{5,4},{6,5},{7,6},{9,8},{10,9},{11,10},{13,12},{... | collective-permute-start | bytes 6152 | tf_op jit(solution)/shard_map/ppermute | solution.py:22
  18.7 9.4 %copy-start = (bf16[1024,2,256]{2,1,0:T(2,128)(2,1)S(1)}, bf16[1024,2,256]{2,1,0:T(2,128)(2,1)}, u32[]{:S(2)}) copy-start(bf16[1024,2,256]{2,1,0:T(2,128)(2,1)} %param.6) | copy-start | bytes 3145732
  18.8 9.4 %collective-permute-start.3 = (f32[1,2,256]{2,1,0:T(2,128)S(1)}, f32[1,2,256]{2,1,0:T(2,128)S(1)}, u32[]{:S(2)}, u32[]{:S(2)}) collective-permute-start(f32[1,2,256]{2,1,0:T(2,128)S(1)} %get-tuple-element.44), channel_id=1, source_target_pairs={{0,1},{1,2},{2,3},{4,5},{5,6},{6,7},{8,9},{9,10},{10,11},{12,13},{... | collective-permute-start | bytes 6152 | tf_op jit(solution)/shard_map/ppermute | solution.py:19
  35.8 7.1 %collective-permute-start.4 = (f32[1,2,256]{2,1,0:T(2,128)S(1)}, f32[1,2,256]{2,1,0:T(2,128)S(1)}, u32[]{:S(2)}, u32[]{:S(2)}) collective-permute-start(f32[1,2,256]{2,1,0:T(2,128)S(1)} %get-tuple-element.39), channel_id=1, source_target_pairs={{1,0},{2,1},{3,2},{5,4},{6,5},{7,6},{9,8},{10,9},{11,10},{13,12},{... | collective-permute-start | bytes 6152 | tf_op jit(solution)/shard_map/ppermute | solution.py:22
  37.7 5.9 %collective-permute-start.5 = (f32[1,2,256]{2,1,0:T(2,128)S(1)}, f32[1,2,256]{2,1,0:T(2,128)S(1)}, u32[]{:S(2)}, u32[]{:S(2)}) collective-permute-start(f32[1,2,256]{2,1,0:T(2,128)S(1)} %get-tuple-element.40), channel_id=1, source_target_pairs={{0,1},{1,2},{2,3},{4,5},{5,6},{6,7},{8,9},{9,10},{10,11},{12,13},{... | collective-permute-start | bytes 6152 | tf_op jit(solution)/shard_map/ppermute | solution.py:19
  49.9 7.6 %collective-permute-start.6 = (f32[1,2,256]{2,1,0:T(2,128)S(1)}, f32[1,2,256]{2,1,0:T(2,128)S(1)}, u32[]{:S(2)}, u32[]{:S(2)}) collective-permute-start(f32[1,2,256]{2,1,0:T(2,128)S(1)} %get-tuple-element.37), channel_id=1, source_target_pairs={{1,0},{2,1},{3,2},{5,4},{6,5},{7,6},{9,8},{10,9},{11,10},{13,12},{... | collective-permute-start | bytes 6152 | tf_op jit(solution)/shard_map/ppermute | solution.py:22
  51.8 20.4 %copy-start.9 = (s32[64]{0:T(128)S(1)}, s32[64]{0:T(128)}, u32[]{:S(2)}) copy-start(s32[64]{0:T(128)} %param.9) | copy-start | bytes 772
  51.8 6.4 %collective-permute-start.7 = (f32[1,2,256]{2,1,0:T(2,128)S(1)}, f32[1,2,256]{2,1,0:T(2,128)S(1)}, u32[]{:S(2)}, u32[]{:S(2)}) collective-permute-start(f32[1,2,256]{2,1,0:T(2,128)S(1)} %get-tuple-element.38), channel_id=1, source_target_pairs={{0,1},{1,2},{2,3},{4,5},{5,6},{6,7},{8,9},{9,10},{10,11},{12,13},{... | collective-permute-start | bytes 6152 | tf_op jit(solution)/shard_map/ppermute | solution.py:19
  64.6 7.6 %collective-permute-start.8 = (f32[1,2,256]{2,1,0:T(2,128)S(1)}, f32[1,2,256]{2,1,0:T(2,128)S(1)}, u32[]{:S(2)}, u32[]{:S(2)}) collective-permute-start(f32[1,2,256]{2,1,0:T(2,128)S(1)} %get-tuple-element.35), channel_id=1, source_target_pairs={{1,0},{2,1},{3,2},{5,4},{6,5},{7,6},{9,8},{10,9},{11,10},{13,12},{... | collective-permute-start | bytes 6152 | tf_op jit(solution)/shard_map/ppermute | solution.py:22
  66.5 6.4 %collective-permute-start.9 = (f32[1,2,256]{2,1,0:T(2,128)S(1)}, f32[1,2,256]{2,1,0:T(2,128)S(1)}, u32[]{:S(2)}, u32[]{:S(2)}) collective-permute-start(f32[1,2,256]{2,1,0:T(2,128)S(1)} %get-tuple-element.36), channel_id=1, source_target_pairs={{0,1},{1,2},{2,3},{4,5},{5,6},{6,7},{8,9},{9,10},{10,11},{12,13},{... | collective-permute-start | bytes 6152 | tf_op jit(solution)/shard_map/ppermute | solution.py:19
  79.2 8.7 %collective-permute-start.10 = (f32[1,2,256]{2,1,0:T(2,128)S(1)}, f32[1,2,256]{2,1,0:T(2,128)S(1)}, u32[]{:S(2)}, u32[]{:S(2)}) collective-permute-start(f32[1,2,256]{2,1,0:T(2,128)S(1)} %get-tuple-element.33), channel_id=1, source_target_pairs={{1,0},{2,1},{3,2},{5,4},{6,5},{7,6},{9,8},{10,9},{11,10},{13,12},{... | collective-permute-start | bytes 6152 | tf_op jit(solution)/shard_map/ppermute | solution.py:22
  81.2 6.8 %collective-permute-start.11 = (f32[1,2,256]{2,1,0:T(2,128)S(1)}, f32[1,2,256]{2,1,0:T(2,128)S(1)}, u32[]{:S(2)}, u32[]{:S(2)}) collective-permute-start(f32[1,2,256]{2,1,0:T(2,128)S(1)} %get-tuple-element.34), channel_id=1, source_target_pairs={{0,1},{1,2},{2,3},{4,5},{5,6},{6,7},{8,9},{9,10},{10,11},{12,13},{... | collective-permute-start | bytes 6152 | tf_op jit(solution)/shard_map/ppermute | solution.py:19
  94.3 7.3 %collective-permute-start.12 = (f32[1,2,256]{2,1,0:T(2,128)S(1)}, f32[1,2,256]{2,1,0:T(2,128)S(1)}, u32[]{:S(2)}, u32[]{:S(2)}) collective-permute-start(f32[1,2,256]{2,1,0:T(2,128)S(1)} %get-tuple-element.31), channel_id=1, source_target_pairs={{1,0},{2,1},{3,2},{5,4},{6,5},{7,6},{9,8},{10,9},{11,10},{13,12},{... | collective-permute-start | bytes 6152 | tf_op jit(solution)/shard_map/ppermute | solution.py:22
  96.2 6.0 %collective-permute-start.13 = (f32[1,2,256]{2,1,0:T(2,128)S(1)}, f32[1,2,256]{2,1,0:T(2,128)S(1)}, u32[]{:S(2)}, u32[]{:S(2)}) collective-permute-start(f32[1,2,256]{2,1,0:T(2,128)S(1)} %get-tuple-element.32), channel_id=1, source_target_pairs={{0,1},{1,2},{2,3},{4,5},{5,6},{6,7},{8,9},{9,10},{10,11},{12,13},{... | collective-permute-start | bytes 6152 | tf_op jit(solution)/shard_map/ppermute | solution.py:19
  109.3 8.9 %copy-start.2 = (bf16[1,32,64,256]{3,2,1,0:T(8,128)(2,1)S(1)}, bf16[1,32,64,256]{3,2,1,0:T(8,128)(2,1)}, u32[]{:S(2)}) copy-start(bf16[1,32,64,256]{3,2,1,0:T(8,128)(2,1)} %param.10) | copy-start | bytes 3145732
  109.3 8.9 %copy-start.7 = (f32[256]{0:T(256)S(1)}, f32[256]{0:T(256)}, u32[]{:S(2)}) copy-start(f32[256]{0:T(256)} %param.11) | copy-start | bytes 3076
  109.3 23.8 %all-to-all-start = ((bf16[1024,2,256]{2,1,0:T(2,128)(2,1)}), bf16[1024,2,256]{2,1,0:T(2,128)(2,1)S(1)}, u32[]{:S(2)}, u32[]{:S(2)}) async-start(bf16[1024,2,256]{2,1,0:T(2,128)(2,1)} %fusion.39), calls=%async_computation | async-start | bytes 2097152 | tf_op jit(solution)/shard_map/all_to_all | solution.py:42
  118.1 164.9 %all-reduce.3.cloned.1.call-start = ((), (), s32[]{:S(2)}) async-start(), calls=%async_computation.1 | async-start | bytes 2097152 | tf_op jit(solution)/shard_map/psum | solution.py:50
  283.0 1.8 copy-start.1
  368.6 55.7 %copy-start.3 = (f32[512,512]{1,0:T(8,128)S(1)}, f32[512,512]{1,0:T(8,128)}, u32[]{:S(2)}) copy-start(f32[512,512]{1,0:T(8,128)} %fusion.61) | copy-start | bytes 3145732
  424.0 3.3 copy-start.5
  427.7 4.2 copy-start.4
Sparse Core Ops, SparseCore 0:
  137.0 145.9 all-reduce.2
where the time goes:
time: 451 us; the launch traced here: 443 us
  other arithmetic  170 us (38%)
  waiting for transfers between devices  160 us (35%)
  starting transfers between devices  61.3 us (14%)
  local copies, waits for them, and re-layouts  19.5 us (4%)
  between operations  18 us (4%)
  matrix products  14.6 us (3%)
    psum x1, waiting for transfers between devices, body(): gram_sum = lax.psum(gram_local, ('cable', 'seg'))  144 us
    another operation x14, other arithmetic, body(): lower_chol = jnp.linalg.cholesky(gram_sum)  78.7 us
    another operation x3, other arithmetic, body(): jax.scipy.linalg.solve_triangular(lower_chol, identity_m, lower=True)  41.4 us
    ppermute x7, starting transfers between devices, padded_2(): lax.ppermute(lax.slice_in_dim(block, block.shape[dim] - width, None, axis...  37.6 us
    div x5, other arithmetic, body(): (source + stiffness * (right_weight * padded[2:] + left_weight * padded[:...  32.8 us
    ppermute x7, starting transfers between devices, padded_2(): lax.ppermute(lax.slice_in_dim(block, 0, width, axis=dim), axis, backward)  14.8 us
    another operation x12, local copies, waits for them, and re-layouts  14 us
    all_to_all x1, waiting for transfers between devices, body(): lax.all_to_all(solved, 'cable', split_axis=0, concat_axis=1, tiled=True)  13.4 us
  transfers between devices with their start and end apart: 16, of which 6 were waited for; matrix products, arithmetic and copies ran while one was open for 2% of the time, Pallas kernels for 0%

commit v1 on v0

v1 whole, which is shorter than its diff:
```python
import jax
import jax.numpy as jnp
from jax import lax
from jax.experimental import pallas as pl
from jax.experimental.pallas import tpu as pltpu
from jax.sharding import PartitionSpec as P

K = 256
SNAP = 256
SWEEPS = 6
DRAG_RATE = 0.1
STRIPS = 8
EDGE = 16
MESH = pl.DeviceIdType.MESH
HI = lax.Precision.HIGHEST
VMEM = pltpu.VMEM
F32 = jnp.float32
BF16 = jnp.bfloat16


def vmem_spec():
    return pl.BlockSpec(memory_space=pltpu.VMEM)


def nt(a, b, precision=None):
    return lax.dot_general(a, b, (((1,), (1,)), ((), ())), precision=precision, preferred_element_type=F32)


def nn(a, b, precision=None):
    return lax.dot_general(a, b, (((1,), (0,)), ((), ())), precision=precision, preferred_element_type=F32)


def tn(a, b, precision=None):
    return lax.dot_general(a, b, (((0,), (0,)), ((), ())), precision=precision, preferred_element_type=F32)


def greet(n_cable, n_seg):
    cable, seg = lax.axis_index("cable"), lax.axis_index("seg")
    barrier = pltpu.get_barrier_semaphore()

    def hail_cable(d, _):
        peer = lax.rem(cable + d, n_cable)
        pl.semaphore_signal(barrier, inc=1, device_id=(peer, seg), device_id_type=MESH)
        return 0

    def hail_seg(d, _):
        peer = lax.rem(seg + d, n_seg)
        pl.semaphore_signal(barrier, inc=1, device_id=(cable, peer), device_id_type=MESH)
        return 0

    lax.fori_loop(1, n_cable, hail_cable, 0)
    lax.fori_loop(1, n_seg, hail_seg, 0)
    pl.semaphore_wait(barrier, n_cable + n_seg - 2)


def relax_kernel(n_cable, n_seg, frames, tension, stiff, arrived,
                 padded, halo, tens_halo, tens_rows, weights, solved32, solved,
                 halo_send, halo_recv, send_sem, recv_sem):
    cable, seg = lax.axis_index("cable"), lax.axis_index("seg")
    nodes = frames.shape[0]
    strip = nodes // STRIPS
    block = nodes // n_cable
    greet(n_cable, n_seg)

    def halo_copies(side):
        peer = seg + 1 if side == 0 else seg - 1
        start = nodes - EDGE if side == 0 else 0
        lane = nodes - 128 if side == 0 else 0
        return [
            pltpu.make_async_remote_copy(
                src_ref=frames.at[pl.ds(start, EDGE), :], dst_ref=halo.at[side],
                send_sem=halo_send.at[side], recv_sem=halo_recv.at[side],
                device_id=(cable, peer), device_id_type=MESH),
            pltpu.make_async_remote_copy(
                src_ref=tension.at[:, pl.ds(lane, 128)], dst_ref=tens_halo.at[side],
                send_sem=halo_send.at[2 + side], recv_sem=halo_recv.at[2 + side],
                device_id=(cable, peer), device_id_type=MESH),
        ]

    @pl.when(seg < n_seg - 1)
    def _():
        for copy in halo_copies(0):
            copy.start()

    @pl.when(seg > 0)
    def _():
        for copy in halo_copies(1):
            copy.start()

    for tile in range(4):
        padded[tile, EDGE:EDGE + nodes, :] = frames[:, tile * 128:(tile + 1) * 128].astype(F32)
    for q in range(2):
        for s in range(STRIPS):
            tens_rows[q, 8 + s:9 + s, :] = tension[q:q + 1, s * strip:(s + 1) * strip]

    @pl.when(seg == 0)
    def _():
        halo[0] = jnp.zeros_like(halo[0])
        tens_halo[0] = jnp.zeros_like(tens_halo[0])

    @pl.when(seg == n_seg - 1)
    def _():
        halo[1] = jnp.zeros_like(halo[1])
        tens_halo[1] = jnp.zeros_like(tens_halo[1])

    @pl.when(seg > 0)
    def _():
        for copy in halo_copies(0):
            copy.wait_recv()

    @pl.when(seg < n_seg - 1)
    def _():
        for copy in halo_copies(1):
            copy.wait_recv()

    for tile in range(4):
        cols = slice(tile * 128, (tile + 1) * 128)
        padded[tile, 0:EDGE, :] = halo[0, :, cols].astype(F32)
        padded[tile, EDGE + nodes:, :] = halo[1, :, cols].astype(F32)
    reach = SWEEPS
    steps = strip + 2 * reach
    full = (STRIPS, 128)
    sub = lax.broadcasted_iota(jnp.int32, full, 0)
    lane = lax.broadcasted_iota(jnp.int32, full, 1)
    low_out = jnp.logical_and(sub == 0, seg == 0)
    high_out = jnp.logical_and(sub == STRIPS - 1, seg == n_seg - 1)
    for q in range(2):
        tens_rows[q, 7:8, :] = tens_halo[0, q:q + 1, :]
        tens_rows[q, 16:17, :] = tens_halo[1, q:q + 1, :]
        before, here, after = (tens_rows[q, 7 + i:15 + i, :] for i in range(3))

        def next_lane(x, y):
            return jnp.where(lane == 127, pltpu.roll(y, 127, 1), pltpu.roll(x, 127, 1))

        def prev_lane(x, y):
            return jnp.where(lane == 0, pltpu.roll(x, 1, 1), pltpu.roll(y, 1, 1))

        right = [0.5 * (before + next_lane(before, here)), 0.5 * (here + next_lane(here, after)),
                 0.5 * (after + next_lane(after, after))]
        left = [prev_lane(before, right[0]), prev_lane(right[0], right[1]), prev_lane(right[1], right[2])]
        for kind, rows in enumerate((left, right)):
            rows[0] = jnp.where(low_out, 0.0, rows[0])
            rows[2] = jnp.where(high_out, 0.0, rows[2])
            for step in range(steps):
                part, at = divmod(128 + step - reach, 128)
                weights[q, kind, step] = jnp.broadcast_to(rows[part][:, at:at + 1], full)

    def piece(q, peer, d):
        return pltpu.make_async_remote_copy(
            src_ref=solved.at[q, pl.ds(pl.multiple_of(peer * block, block), block), :],
            dst_ref=arrived.at[2 * cable + q],
            send_sem=send_sem.at[q, d], recv_sem=recv_sem.at[2 * cable + q],
            device_id=(peer, seg), device_id_type=MESH)

    for q in range(2):
        scale = [jnp.broadcast_to(stiff[0:1, h * 128:(h + 1) * 128], full) for h in range(2)]

        def advance(step, levels, coefs):
            lw, rw = weights[q, 0, step], weights[q, 1, step]
            total = lw + rw
            out = []
            for h in range(2):
                value = padded[2 * q + h, pl.ds(EDGE - reach + step, STRIPS, stride=strip), :]
                inv = 1.0 / (1.0 + scale[h] * total)
                si = scale[h] * inv
                coefs[h].append((si * lw, si * rw, value * inv))
                levels[h][0].append(value)
                for k in range(1, SWEEPS + 1):
                    below, above, own = coefs[h][-1 - k]
                    value = own + (above * levels[h][k - 1][-1] + below * levels[h][k - 1][-3])
                    levels[h][k].append(value)
                coefs[h][:] = coefs[h][-(SWEEPS + 1):]
                for k in range(SWEEPS + 1):
                    levels[h][k][:] = levels[h][k][-2:] if k < SWEEPS else levels[h][k][-1:]
                out.append(levels[h][SWEEPS][-1])
            return out

        zero = jnp.zeros(full, F32)
        levels = [[[zero, zero] for _ in range(SWEEPS)] + [[zero]] for _ in range(2)]
        coefs = [[(zero, zero, zero)] * (SWEEPS + 1) for _ in range(2)]
        for step in range(2 * reach):
            advance(step, levels, coefs)

        unroll = 8

        def turn(i, carry):
            levels, coefs = jax.tree.map(lambda x: x, carry)
            levels = [[list(x) for x in lv] for lv in levels]
            coefs = [[tuple(x) for x in cf] for cf in coefs]
            for u in range(unroll):
                row = i * unroll + u
                out = advance(2 * reach + row, levels, coefs)
                for h in range(2):
                    solved32[h, pl.ds(row, STRIPS, stride=strip), :] = out[h]
            return levels, coefs

        lax.fori_loop(0, strip // unroll, turn, (levels, coefs))
        for h in range(2):
            solved[q, :, h * 128:(h + 1) * 128] = solved32[h].astype(BF16)

        def send(d, _):
            piece(q, lax.rem(cable + d, n_cable), d).start()
            return 0

        lax.fori_loop(1, n_cable, send, 0)
        arrived[2 * cable + q] = solved[q, pl.ds(pl.multiple_of(cable * block, block), block), :]

    def await_piece(d, _):
        peer = lax.rem(cable + d, n_cable)
        for q in range(2):
            pltpu.make_async_remote_copy(
                src_ref=solved.at[q, pl.ds(0, block), :], dst_ref=arrived.at[2 * peer + q],
                send_sem=send_sem.at[q, d], recv_sem=recv_sem.at[2 * peer + q],
                device_id=(peer, seg), device_id_type=MESH).wait_recv()
            piece(q, peer, d).wait_send()
        return 0

    lax.fori_loop(1, n_cable, await_piece, 0)

    @pl.when(seg < n_seg - 1)
    def _():
        for copy in halo_copies(0):
            copy.wait_send()

    @pl.when(seg > 0)
    def _():
        for copy in halo_copies(1):
            copy.wait_send()


def relax_and_exchange(frames, tension, stiff):
    n_cable, n_seg = lax.axis_size("cable"), lax.axis_size("seg")
    nodes = frames.shape[0]
    steps = nodes // STRIPS + 2 * SWEEPS
    dma = pltpu.SemaphoreType.DMA
    return pl.pallas_call(
        lambda *refs: relax_kernel(n_cable, n_seg, *refs),
        out_shape=jax.ShapeDtypeStruct((2 * n_cable, nodes // n_cable, SNAP), BF16),
        in_specs=[vmem_spec()] * 3,
        out_specs=vmem_spec(),
        scratch_shapes=[
            VMEM((4, nodes + 2 * EDGE, 128), F32),
            VMEM((2, EDGE, 2 * SNAP), BF16),
            VMEM((2, 2, 128), F32),
            VMEM((2, 24, 128), F32),
            VMEM((2, 2, steps, STRIPS, 128), F32),
            VMEM((2, nodes, 128), F32),
            VMEM((2, nodes, SNAP), BF16),
            dma((4,)), dma((4,)), dma((2, n_cable)), dma((2 * n_cable,)),
        ],
        compiler_params=pltpu.CompilerParams(collective_id=0, has_side_effects=True, vmem_limit_bytes=40 * 2**20),
        name="relax_exchange",
    )(frames, tension, stiff)


def reduce_kernel(n_cable, n_seg, local, total, parts, sums, send1, recv1, send2, recv2, send3, recv3):
    cable, seg = lax.axis_index("cable"), lax.axis_index("seg")
    depth = local.shape[0] // n_cable
    greet(n_cable, n_seg)

    def rows(i):
        return pl.ds(pl.multiple_of(i * depth, depth), depth)

    def scatter(d):
        peer = lax.rem(cable + d, n_cable)
        return pltpu.make_async_remote_copy(
            src_ref=local.at[rows(peer), :], dst_ref=parts.at[cable], send_sem=send1.at[d], recv_sem=recv1.at[cable],
            device_id=(peer, seg), device_id_type=MESH)

    def scattered(d):
        peer = lax.rem(cable + d, n_cable)
        return pltpu.make_async_remote_copy(
            src_ref=local.at[rows(peer), :], dst_ref=parts.at[peer], send_sem=send1.at[d], recv_sem=recv1.at[peer],
            device_id=(peer, seg), device_id_type=MESH)

    def swap(d):
        peer = lax.rem(seg + d, n_seg)
        return pltpu.make_async_remote_copy(
            src_ref=sums.at[seg], dst_ref=sums.at[seg], send_sem=send2.at[d], recv_sem=recv2.at[seg],
            device_id=(cable, peer), device_id_type=MESH)

    def swapped(d):
        peer = lax.rem(seg + d, n_seg)
        return pltpu.make_async_remote_copy(
            src_ref=sums.at[seg], dst_ref=sums.at[peer], send_sem=send2.at[d], recv_sem=recv2.at[peer],
            device_id=(cable, peer), device_id_type=MESH)

    def gather(d):
        peer = lax.rem(cable + d, n_cable)
        return pltpu.make_async_remote_copy(
            src_ref=total.at[rows(cable), :], dst_ref=total.at[rows(cable), :], send_sem=send3.at[d],
            recv_sem=recv3.at[cable], device_id=(peer, seg), device_id_type=MESH)

    def gathered(d):
        peer = lax.rem(cable + d, n_cable)
        return pltpu.make_async_remote_copy(
            src_ref=total.at[rows(peer), :], dst_ref=total.at[rows(peer), :], send_sem=send3.at[d],
            recv_sem=recv3.at[peer], device_id=(peer, seg), device_id_type=MESH)

    def each(first, last, act):
        def turn(d, _):
            act(d)
            return 0
        lax.fori_loop(first, last, turn, 0)

    each(1, n_cable, lambda d: scatter(d).start())
    parts[cable] = local[rows(cable), :]
    each(1, n_cable, lambda d: scattered(d).wait_recv())
    acc = parts[0]
    for i in range(1, n_cable):
        acc = acc + parts[i]
    sums[seg] = acc
    each(1, n_seg, lambda d: swap(d).start())
    each(1, n_seg, lambda d: swapped(d).wait_recv())
    acc = sums[0]
    for i in range(1, n_seg):
        acc = acc + sums[i]
    total[rows(cable), :] = acc
    each(1, n_cable, lambda d: gather(d).start())
    each(1, n_cable, lambda d: gathered(d).wait_recv())
    each(1, n_cable, lambda d: scatter(d).wait_send())
    each(1, n_seg, lambda d: swap(d).wait_send())
    each(1, n_cable, lambda d: gather(d).wait_send())


def all_reduce(local):
    n_cable, n_seg = lax.axis_size("cable"), lax.axis_size("seg")
    rows, cols = local.shape
    depth = rows // n_cable
    dma = pltpu.SemaphoreType.DMA
    return pl.pallas_call(
        lambda *refs: reduce_kernel(n_cable, n_seg, *refs),
        out_shape=jax.ShapeDtypeStruct((rows, cols), F32),
        in_specs=[vmem_spec()],
        out_specs=vmem_spec(),
        scratch_shapes=[
            VMEM((n_cable, depth, cols), F32), VMEM((n_seg, depth, cols), F32),
            dma((n_cable,)), dma((n_cable,)), dma((n_seg,)), dma((n_seg,)), dma((n_cable,)), dma((n_cable,)),
        ],
        compiler_params=pltpu.CompilerParams(collective_id=1, has_side_effects=True, vmem_limit_bytes=40 * 2**20),
        name="gram_reduce",
    )(local)


def gram_kernel(owner, basis, singular, arrived, gram, ordered, by_position, staged):
    positions, block = arrived.shape[0], arrived.shape[1]
    for p in range(positions):
        rows = arrived[owner[p]].astype(F32)
        for h in range(2):
            by_position[h, p * block:(p + 1) * block, :] = rows[:, h * 128:(h + 1) * 128]

    def spread(n, _):
        for h in range(2):
            part = by_position[h, pl.ds(n, positions, stride=block), :]
            ordered[pl.ds(pl.multiple_of(n * positions, positions), positions), h * 128:(h + 1) * 128] = (
                part.astype(BF16))
        return 0

    lax.fori_loop(0, block, spread, 0)
    scaled = (basis[...].astype(F32) * singular[...]).astype(BF16)
    staged[...] = scaled
    snaps = ordered[...]
    gram[0:K, :] = tn(scaled, scaled)
    gram[K:2 * K, :] = tn(snaps, scaled)
    gram[2 * K:, :] = tn(snaps, snaps)


def gram_blocks(owner_map, basis, singular, arrived):
    rows = basis.shape[0]
    return pl.pallas_call(
        gram_kernel,
        out_shape=[jax.ShapeDtypeStruct((3 * K, K), F32), jax.ShapeDtypeStruct((rows, SNAP), BF16)],
        in_specs=[pl.BlockSpec(memory_space=pltpu.SMEM)] + [vmem_spec()] * 3,
        out_specs=[vmem_spec()] * 2,
        scratch_shapes=[VMEM((2, rows, 128), F32), VMEM((rows, K), BF16)],
        compiler_params=pltpu.CompilerParams(vmem_limit_bytes=40 * 2**20),
        name="gram_blocks",
    )(owner_map, basis, singular, arrived)


def factor_128(a, upper, inverse):
    size, n = 8, 16
    full = (size, 128)
    rows = lax.broadcasted_iota(jnp.int32, full, 0)
    lanes = lax.broadcasted_iota(jnp.int32, full, 1)
    a = list(a)
    q = [jnp.where(lanes == rows + size * t, 1.0, 0.0) for t in range(n)]
    for kb in range(n):
        at = size * kb
        r = [jnp.broadcast_to(a[kb][k:k + 1, :], full) for k in range(size)]
        s = [jnp.broadcast_to(q[kb][k:k + 1, :], full) for k in range(size)]
        col = {t: [jnp.broadcast_to(a[t][:, at + k:at + k + 1], full) for k in range(size)]
               for t in range(kb + 1, n)}
        e, m, pivot = {}, {}, []
        for j in range(size):
            own = jnp.broadcast_to(a[kb][:, at + j:at + j + 1], full)
            for i in range(j, size):
                e[i, j] = jnp.broadcast_to(own[i:i + 1, :], full)
        for k in range(size):
            pivot.append(1.0 / e[k, k])
            for i in range(k + 1, size):
                m[i, k] = e[i, k] * pivot[k]
            for i in range(k + 1, size):
                for j in range(k + 1, i + 1):
                    e[i, j] = e[i, j] - m[i, k] * e[j, k]
                r[i] = r[i] - m[i, k] * r[k]
                s[i] = s[i] - m[i, k] * s[k]
        z = [r[k] * pivot[k] for k in range(size)]
        zs = [s[k] * pivot[k] for k in range(size)]
        for k in reversed(range(size)):
            for j in range(k):
                z[j] = z[j] - m[k, j] * z[k]
                zs[j] = zs[j] - m[k, j] * zs[k]
        for t in range(kb + 1, n):
            for k in range(size):
                a[t] = a[t] - col[t][k] * z[k]
                q[t] = q[t] - col[t][k] * zs[k]
        ut, wt = jnp.zeros(full, F32), jnp.zeros(full, F32)
        for k in range(size):
            root = lax.rsqrt(e[k, k])
            ut = jnp.where(rows == k, r[k] * root, ut)
            wt = jnp.where(rows == k, s[k] * root, wt)
        upper[at:at + size, :] = jnp.where(lanes >= rows + at, ut, 0.0)
        inverse[at:at + size, :] = jnp.where(lanes <= rows + at, wt, 0.0)


def factor_256(a, upper, inverse):
    h = 128
    factor_128([a[8 * t:8 * t + 8, :h] for t in range(16)], upper.at[:h, :h], inverse.at[:h, :h])
    w1 = inverse[:h, :h]
    low = nt(a[h:, :h], w1, HI)
    upper[:h, h:] = low.T
    upper[h:, :h] = jnp.zeros((h, h), F32)
    inverse[:h, h:] = jnp.zeros((h, h), F32)
    a[h:, h:] = a[h:, h:] - nt(low, low, HI)
    t = nn(low, w1, HI)
    factor_128([a[h + 8 * t:h + 8 * t + 8, h:] for t in range(16)], upper.at[h:, h:], inverse.at[h:, h:])
    inverse[h:, :h] = -nn(inverse[h:, h:], t, HI)


def factor_kernel(rows_all, gram, basis, singular, snaps, factor, new_basis, a, inv1, inv2):
    scale = 1.0 / rows_all
    a[...] = gram[0:K, :] * scale
    factor_256(a, factor.at[:K, :K], inv1)
    w1 = inv1[...]
    low = nt(gram[K:2 * K, :] * scale, w1, HI)
    factor[:K, K:] = low.T
    factor[K:, :K] = jnp.zeros((K, K), F32)
    a[...] = gram[2 * K:, :] * scale - nt(low, low, HI)
    t = nn(low, w1, HI)
    factor_256(a, factor.at[K:, K:], inv2)
    w2 = inv2[...]
    cross = (-nn(w2, t, HI)).astype(BF16)
    w1b, w2b = w1.astype(BF16), w2.astype(BF16)
    scaled = (basis[...].astype(F32) * singular[...]).astype(BF16)
    new_basis[:, :K] = nt(scaled, w1b).astype(BF16)
    new_basis[:, K:] = (nt(scaled, cross) + nt(snaps[...], w2b)).astype(BF16)


def factor_and_rotate(rows_all, gram, basis, singular, snaps):
    rows, width = basis.shape[0], 2 * K
    return pl.pallas_call(
        lambda *refs: factor_kernel(rows_all, *refs),
        out_shape=[jax.ShapeDtypeStruct((width, width), F32), jax.ShapeDtypeStruct((rows, width), BF16)],
        in_specs=[vmem_spec()] * 4,
        out_specs=[vmem_spec()] * 2,
        scratch_shapes=[VMEM((K, K), F32)] * 3,
        compiler_params=pltpu.CompilerParams(vmem_limit_bytes=40 * 2**20),
        name="factor_rotate",
    )(gram, basis, singular, snaps)


def body(frames, tension, step_index, owner_map, old_basis, singular):
    stiff = (DRAG_RATE * (1.0 + step_index.astype(F32)))[None, :]
    nodes = frames.shape[0]
    arrived = relax_and_exchange(frames.reshape(nodes, 2 * SNAP), tension.T, stiff)
    basis = old_basis.reshape(-1, K)
    gain = singular[None, :]
    local, snaps = gram_blocks(owner_map, basis, gain, arrived)
    gram = all_reduce(local)
    rows_all = basis.shape[0] * lax.axis_size("cable") * lax.axis_size("seg")
    factor, rotated = factor_and_rotate(rows_all, gram, basis, gain, snaps)
    return factor, rotated.reshape(old_basis.shape[:3] + (2 * K,))


def solution(mesh):
    return jax.shard_map(
        body,
        mesh=mesh,
        in_specs=(P("seg", "cable", None), P("seg", "cable"), P(), P(), P("seg", "cable", None, None), P()),
        out_specs=(P(), P("seg", "cable", None, None)),
        check_vma=False,
    )
```

time: 451 us -> 101 us (0.22)
  the two profiles are of different devices: /device:TPU:1 before, /device:TPU:24 now
where the time goes in v1:
time: 101 us
  Pallas kernels  97.7 us (97%)
  local copies, waits for them, and re-layouts  1.55 us (2%)
    pallas_call x1, Pallas kernels, all_reduce(): pl.pallas_call(lambda *refs: reduce_kernel(n_cable, n_seg, *refs), out_sh...  38.8 us
    pallas_call x1, Pallas kernels, relax_and_exchange(): pl.pallas_call(lambda *refs: relax_kernel(n_cable, n_seg, *refs), out_sha...  28.7 us
    pallas_call x1, Pallas kernels, factor_and_rotate(): pl.pallas_call(lambda *refs: factor_kernel(rows_all, *refs), out_shape=[j...  26.2 us
    pallas_call x1, Pallas kernels, gram_blocks(): pl.pallas_call(gram_kernel, out_shape=[jax.ShapeDtypeStruct((3 * K, K), F...  4.03 us

profile of v1, /device:TPU:24, one launch (start us, length us, event | category | flops | bytes accessed | tf_op | source)
XLA Modules:
  0.0 100.7 jit_solution(16890625487835772982)
XLA Ops:
  0.6 0.0 copy-start.1
  0.6 0.7 add_multiply_fusion
  1.3 0.0 copy-start
  1.3 0.0 copy-start.2
  1.3 0.0 copy-start.3
  1.3 1.5 %copy.8 = bf16[128,8,2,256]{3,1,2,0:T(8,128)(2,1)S(1)} copy(bf16[128,8,2,256]{3,2,1,0:T(2,128)(2,1)} %bitcast.14) | data formatting | bytes 2097152
  2.9 0.0 copy-done.1
  2.9 28.7 %relax_exchange.1.arrived = bf16[64,32,256]{2,1,0:T(8,128)(2,1)S(1)} custom-call(bf16[1024,512]{1,0:T(8,128)(2,1)S(1)} %bitcast.9, f32[2,1024]{1,0:T(2,128)S(1)} %bitcast.10, f32[1,256]{1,0:T(1,128)S(1)} %bitcast.13), custom_call_target="tpu_custom_call" | custom-call | tf_op jit(solution)/shard_map/relax_exchange/pallas_call | solution.py:236
  31.6 0.0 copy-done
  31.6 0.0 copy-done.2
  31.6 0.0 copy-done.3
  31.6 4.0 %gram_blocks.1 = (f32[768,256]{1,0:T(8,128)S(1)}, bf16[2048,256]{1,0:T(8,128)(2,1)S(1)}) custom-call(s32[64]{0:T(128)S(1)} %copy-done.3, bf16[2048,256]{1,0:T(8,128)(2,1)S(1)} %bitcast.7, f32[1,256]{1,0:T(1,128)S(1)} %bitcast.11, bf16[64,32,256]{2,1,0:T(8,128)(2,1)S(1)} %relax_exchange.1.arrived), custom_call_target="tpu_custom_call" | custom-call | tf_op jit(solution)/shard_map/gram_blocks/pallas_call | solution.py:370
  35.6 38.8 %gram_reduce.1.refs_0_ = f32[768,256]{1,0:T(8,128)S(1)} custom-call(f32[768,256]{1,0:T(8,128)S(1)} %get-tuple-element.6.refs_0_), custom_call_target="tpu_custom_call" | custom-call | tf_op jit(solution)/shard_map/gram_reduce/pallas_call | solution.py:331
  74.5 26.2 %factor_rotate.1 = (f32[512,512]{1,0:T(8,128)}, bf16[2048,512]{1,0:T(8,128)(2,1)}) custom-call(f32[768,256]{1,0:T(8,128)S(1)} %gram_reduce.1.refs_0_, bf16[2048,256]{1,0:T(8,128)(2,1)S(1)} %bitcast.8, f32[1,256]{1,0:T(1,128)S(1)} %bitcast.12, bf16[2048,256]{1,0:T(8,128)(2,1)S(1)} %get-tuple-element.7.refs_3_), custom_call_target="tpu_custom_call" | custom-call | tf_op jit(solution)/shard_map/factor_rotate/pallas_call | solution.py:462
Async XLA Ops:
  0.6 2.3 %copy-start.1 = (f32[1024,2]{0,1:T(2,128)S(1)}, f32[1024,2]{0,1:T(2,128)}, u32[]{:S(2)}) copy-start(f32[1024,2]{0,1:T(2,128)} %param.7) | copy-start | bytes 24580
  1.3 30.2 %copy-start = (bf16[1,32,64,256]{3,2,1,0:T(8,128)(2,1)S(1)}, bf16[1,32,64,256]{3,2,1,0:T(8,128)(2,1)}, u32[]{:S(2)}) copy-start(bf16[1,32,64,256]{3,2,1,0:T(8,128)(2,1)} %param.10) | copy-start | bytes 3145732
  1.3 30.2 %copy-start.2 = (f32[256]{0:T(256)S(1)}, f32[256]{0:T(256)}, u32[]{:S(2)}) copy-start(f32[256]{0:T(256)} %param.11) | copy-start | bytes 3076
  1.3 30.2 %copy-start.3 = (s32[64]{0:T(128)S(1)}, s32[64]{0:T(128)}, u32[]{:S(2)}) copy-start(s32[64]{0:T(128)} %owner.1) | copy-start | bytes 772

commit v2 on v0

v2 whole, which is shorter than its diff:
```python
import jax
import jax.numpy as jnp
from jax import lax
from jax.experimental import pallas as pl
from jax.experimental.pallas import tpu as pltpu
from jax.sharding import PartitionSpec as P

K = 256
SNAP = 256
SWEEPS = 6
DRAG_RATE = 0.1
STRIPS = 8
EDGE = 16
MESH = pl.DeviceIdType.MESH
HI = lax.Precision.HIGHEST
VMEM = pltpu.VMEM
F32 = jnp.float32
BF16 = jnp.bfloat16


def vmem_spec():
    return pl.BlockSpec(memory_space=pltpu.VMEM)


def nt(a, b, precision=None):
    return lax.dot_general(a, b, (((1,), (1,)), ((), ())), precision=precision, preferred_element_type=F32)


def nn(a, b, precision=None):
    return lax.dot_general(a, b, (((1,), (0,)), ((), ())), precision=precision, preferred_element_type=F32)


def tn(a, b, precision=None):
    return lax.dot_general(a, b, (((0,), (0,)), ((), ())), precision=precision, preferred_element_type=F32)


def place():
    cable, seg = lax.axis_index("cable"), lax.axis_index("seg")
    return cable, seg, cable // 8, lax.rem(cable // 4, 2), lax.rem(cable, 4), seg // 2, lax.rem(seg, 2)


N_CABLE = 32
N_SEG = 4
PLANE = 16


def each(first, last, act):
    def turn(d, _):
        act(d)
        return 0
    lax.fori_loop(first, last, turn, 0)


def greet():
    cable, seg, x, y_lo, z, y_hi, core = place()
    barrier = pltpu.get_barrier_semaphore()

    def hail(device):
        pl.semaphore_signal(barrier, inc=1, device_id=device, device_id_type=MESH)

    each(1, N_CABLE, lambda d: hail((lax.rem(cable + d, N_CABLE), seg)))
    each(1, N_SEG, lambda d: hail((cable, lax.rem(seg + d, N_SEG))))
    hail((x * 8 + (1 - y_lo) * 4 + z, (1 - y_hi) * 2 + core))
    return lambda: pl.semaphore_wait(barrier, N_CABLE + N_SEG - 1)


class Reduce:
    def __init__(self, local, total, half, parts, lines, sems):
        self.local, self.total, self.half, self.parts, self.lines = local, total, half, parts, lines
        self.send, self.recv = sems
        self.rows = local.shape[0]
        self.depth = self.rows // 2 // PLANE
        self.cable, self.seg, self.x, self.y_lo, self.z, self.y_hi, self.core = place()
        self.spot = self.x * 4 + self.z
        self.y = self.y_hi * 2 + self.y_lo
        self.sister = (self.cable, self.y_hi * 2 + 1 - self.core)

    def copy(self, src, dst, slot, landing, device):
        return pltpu.make_async_remote_copy(
            src_ref=src, dst_ref=dst, send_sem=self.send.at[slot], recv_sem=self.recv.at[landing],
            device_id=device, device_id_type=MESH)

    def plane(self, d):
        spot = lax.rem(self.spot + d, PLANE)
        return spot, ((spot // 4) * 8 + self.y_lo * 4 + lax.rem(spot, 4), self.seg)

    def line(self, d):
        y = lax.rem(self.y + d, 4)
        return y, (self.x * 8 + lax.rem(y, 2) * 4 + self.z, (y // 2) * 2 + self.core)

    def part(self, spot):
        at = self.core * (self.rows // 2) + spot * self.depth
        return pl.ds(pl.multiple_of(at, self.depth), self.depth)

    def own_half(self):
        return pl.ds(pl.multiple_of(self.core * (self.rows // 2), self.rows // 2), self.rows // 2)

    def other_half(self):
        return pl.ds(pl.multiple_of((1 - self.core) * (self.rows // 2), self.rows // 2), self.rows // 2)

    def c1(self):
        return self.copy(self.local.at[self.other_half(), :], self.half, 0, 0, self.sister)

    def p1(self, d, mine):
        spot, device = self.plane(d)
        return self.copy(self.half.at[pl.ds(pl.multiple_of(spot * self.depth, self.depth), self.depth), :],
                         self.parts.at[self.spot if mine else spot], 16 + d, 16 + (self.spot if mine else spot), device)

    def l1(self, d, mine):
        y, device = self.line(d)
        return self.copy(self.lines.at[self.y], self.lines.at[self.y if mine else y], 4 + d,
                         4 + (self.y if mine else y), device)

    def p2(self, d, mine):
        spot, device = self.plane(d)
        rows = self.part(self.spot if mine else spot)
        return self.copy(self.total.at[rows, :], self.total.at[rows, :], 32 + d,
                         32 + (self.spot if mine else spot), device)

    def c2(self, mine):
        rows = self.own_half() if mine else self.other_half()
        return self.copy(self.total.at[rows, :], self.total.at[rows, :], 1, 1, self.sister)

    def s0(self):
        self.c1().start()

    def s1(self):
        self.c1().wait_recv()
        self.half[...] = self.half[...] + self.local[self.own_half(), :]
        each(1, PLANE, lambda d: self.p1(d, True).start())
        self.parts[self.spot] = self.half[pl.ds(pl.multiple_of(self.spot * self.depth, self.depth), self.depth), :]

    def s2(self):
        each(1, PLANE, lambda d: self.p1(d, False).wait_recv())
        acc = self.parts[0]
        for i in range(1, PLANE):
            acc = acc + self.parts[i]
        self.lines[self.y] = acc
        each(1, 4, lambda d: self.l1(d, True).start())

    def s3(self):
        each(1, 4, lambda d: self.l1(d, False).wait_recv())
        acc = (self.lines[0] + self.lines[1]) + (self.lines[2] + self.lines[3])
        self.total[self.part(self.spot), :] = acc
        each(1, PLANE, lambda d: self.p2(d, True).start())

    def s4(self):
        each(1, PLANE, lambda d: self.p2(d, False).wait_recv())
        self.c2(True).start()

    def s5(self):
        self.c2(False).wait_recv()

    def drain(self):
        self.c1().wait_send()
        each(1, PLANE, lambda d: self.p1(d, True).wait_send())
        each(1, 4, lambda d: self.l1(d, True).wait_send())
        each(1, PLANE, lambda d: self.p2(d, True).wait_send())
        self.c2(True).wait_send()


def reduce_scratch(rows):
    depth = rows // 2 // PLANE
    return [VMEM((rows // 2, K), F32), VMEM((PLANE, depth, K), F32), VMEM((4, depth, K), F32),
            pltpu.SemaphoreType.DMA((48,)), pltpu.SemaphoreType.DMA((48,))]


def factor_128(a, upper, inverse):
    size, n = 8, 16
    rows = lax.broadcasted_iota(jnp.int32, (size, 128), 0)
    lanes = lax.broadcasted_iota(jnp.int32, (size, 128), 1)
    depth = lax.broadcasted_iota(jnp.int32, (n, size, 128), 0)
    q = jnp.where(lanes[None] == rows[None] + size * depth, 1.0, 0.0).astype(F32)
    for kb in range(n):
        at = size * kb
        own, own_q = a[0], q[0]
        a, q = a[1:], q[1:]
        stack = lambda x: jnp.broadcast_to(x[:, None, :], (size, size, 128))
        rest = n - 1 - kb
        r, s = stack(own), stack(own_q)
        cols = [stack(jnp.broadcast_to(own[:, at + j:at + j + 1], (size, 128))) for j in range(size)]
        side = [jnp.broadcast_to(a[:, :, at + k:at + k + 1], (rest, size, 128)) for k in range(size)] if rest else []
        m, rr, ss, pivot, root = [], [], [], [], []
        ut, wt = jnp.zeros((size, 128), F32), jnp.zeros((size, 128), F32)
        for k in range(size):
            d = cols[k][0]
            pivot.append(1.0 / d)
            rr.append(r[0]); ss.append(s[0])
            if k < size - 1:
                below = cols[k][1:]
                mk = below * pivot[k][None]
                m.append(mk)
                for j in range(k + 1, size):
                    cols[j] = cols[j][1:] if j == k + 1 and False else cols[j][1:] - mk * below[j - k - 1][None]
                r = r[1:] - mk * r[0][None]
                s = s[1:] - mk * s[0][None]
            rt = lax.rsqrt(d)
            ut = jnp.where(rows == k, rr[k] * rt, ut)
            wt = jnp.where(rows == k, ss[k] * rt, wt)
        z, zs = [None] * size, [None] * size
        for k in reversed(range(size)):
            zk, zsk = rr[k] * pivot[k], ss[k] * pivot[k]
            for j in range(k + 1, size):
                zk = zk - m[k][j - k - 1] * z[j]
                zsk = zsk - m[k][j - k - 1] * zs[j]
            z[k], zs[k] = zk, zsk
        if rest:
            for k in range(size):
                a = a - side[k] * z[k][None]
                q = q - side[k] * zs[k][None]
        upper[at:at + size, :] = jnp.where(lanes >= rows + at, ut, 0.0)
        inverse[at:at + size, :] = jnp.where(lanes <= rows + at, wt, 0.0)


def factor_256(a, upper, inverse, between=None):
    h = 128
    factor_128(a[:h, :h].reshape(16, 8, h), upper.at[:h, :h], inverse.at[:h, :h])
    if between is not None:
        between[0]()
    w1 = inverse[:h, :h]
    low = nt(a[h:, :h], w1, HI)
    upper[:h, h:] = low.T
    upper[h:, :h] = jnp.zeros((h, h), F32)
    inverse[:h, h:] = jnp.zeros((h, h), F32)
    a[h:, h:] = a[h:, h:] - nt(low, low, HI)
    t = nn(low, w1, HI)
    if between is not None:
        between[1]()
    factor_128(a[h:, h:].reshape(16, 8, h), upper.at[h:, h:], inverse.at[h:, h:])
    if between is not None:
        between[2]()
    inverse[h:, :h] = -nn(inverse[h:, h:], t, HI)


class Halo:
    def __init__(self, frames, tension, halo, tens_halo, send, recv):
        self.refs = frames, tension, halo, tens_halo, send, recv
        self.cable, self.seg = lax.axis_index("cable"), lax.axis_index("seg")

    def copies(self, side):
        frames, tension, halo, tens_halo, send, recv = self.refs
        nodes = frames.shape[0]
        peer = self.seg + 1 if side == 0 else self.seg - 1
        return [
            pltpu.make_async_remote_copy(
                src_ref=frames.at[pl.ds(nodes - EDGE if side == 0 else 0, EDGE), :], dst_ref=halo.at[side],
                send_sem=send.at[side], recv_sem=recv.at[side],
                device_id=(self.cable, peer), device_id_type=MESH),
            pltpu.make_async_remote_copy(
                src_ref=tension.at[:, pl.ds(nodes - 128 if side == 0 else 0, 128)], dst_ref=tens_halo.at[side],
                send_sem=send.at[2 + side], recv_sem=recv.at[2 + side],
                device_id=(self.cable, peer), device_id_type=MESH),
        ]

    def guarded(self, sends, act):
        for side in range(2):
            has_right, has_left = self.seg < N_SEG - 1, self.seg > 0
            here = (has_right, has_left) if sends else (has_left, has_right)

            @pl.when(here[side])
            def _():
                for copy in self.copies(side):
                    act(copy)

    def start(self):
        self.guarded(True, lambda copy: copy.start())

    def wait_recv(self):
        self.guarded(False, lambda copy: copy.wait_recv())

    def wait_send(self):
        self.guarded(True, lambda copy: copy.wait_send())

    def zero_ends(self):
        halo, tens_halo = self.refs[2:4]

        @pl.when(self.seg == 0)
        def _():
            halo[0] = jnp.zeros_like(halo[0])
            tens_halo[0] = jnp.zeros_like(tens_halo[0])

        @pl.when(self.seg == N_SEG - 1)
        def _():
            halo[1] = jnp.zeros_like(halo[1])
            tens_halo[1] = jnp.zeros_like(tens_halo[1])


def make_weights(seg, tens_halo, tens_rows, weights, steps):
    reach = SWEEPS
    full = (STRIPS, 128)
    sub = lax.broadcasted_iota(jnp.int32, full, 0)
    lane = lax.broadcasted_iota(jnp.int32, full, 1)
    low_out = jnp.logical_and(sub == 0, seg == 0)
    high_out = jnp.logical_and(sub == STRIPS - 1, seg == N_SEG - 1)
    for q in range(2):
        tens_rows[q, 7:8, :] = tens_halo[0, q:q + 1, :]
        tens_rows[q, 16:17, :] = tens_halo[1, q:q + 1, :]
        before, here, after = (tens_rows[q, 7 + i:15 + i, :] for i in range(3))

        def next_lane(x, y):
            return jnp.where(lane == 127, pltpu.roll(y, 127, 1), pltpu.roll(x, 127, 1))

        def prev_lane(x, y):
            return jnp.where(lane == 0, pltpu.roll(x, 1, 1), pltpu.roll(y, 1, 1))

        right = [0.5 * (before + next_lane(before, here)), 0.5 * (here + next_lane(here, after)),
                 0.5 * (after + next_lane(after, after))]
        left = [prev_lane(before, right[0]), prev_lane(right[0], right[1]), prev_lane(right[1], right[2])]
        for kind, rows in enumerate((left, right)):
            rows[0] = jnp.where(low_out, 0.0, rows[0])
            rows[2] = jnp.where(high_out, 0.0, rows[2])
            for step in range(steps):
                part, at = divmod(128 + step - reach, 128)
                weights[q, kind, step] = jnp.broadcast_to(rows[part][:, at:at + 1], full)


def relax(q, scale, padded, weights, solved32, solved, strip, block):
    reach = SWEEPS
    full = (STRIPS, 128)

    def advance(step, levels, coefs):
        lw, rw = weights[q, 0, step], weights[q, 1, step]
        total = lw + rw
        out = []
        for h in range(2):
            value = padded[2 * q + h, pl.ds(EDGE - reach + step, STRIPS, stride=strip), :]
            inv = 1.0 / (1.0 + scale[h] * total)
            si = scale[h] * inv
            coefs[h].append((si * lw, si * rw, value * inv))
            levels[h][0].append(value)
            for k in range(1, SWEEPS + 1):
                below, above, own = coefs[h][-1 - k]
                value = own + (above * levels[h][k - 1][-1] + below * levels[h][k - 1][-3])
                levels[h][k].append(value)
            coefs[h][:] = coefs[h][-(SWEEPS + 1):]
            for k in range(SWEEPS + 1):
                levels[h][k][:] = levels[h][k][-2:] if k < SWEEPS else levels[h][k][-1:]
            out.append(levels[h][SWEEPS][-1])
        return out

    zero = jnp.zeros(full, F32)
    levels = [[[zero, zero] for _ in range(SWEEPS)] + [[zero]] for _ in range(2)]
    coefs = [[(zero, zero, zero)] * (SWEEPS + 1) for _ in range(2)]
    for step in range(2 * reach):
        advance(step, levels, coefs)
    unroll = 8

    def turn(i, carry):
        levels, coefs = carry
        levels = [[list(x) for x in lv] for lv in levels]
        coefs = [[tuple(x) for x in cf] for cf in coefs]
        for u in range(unroll):
            row = i * unroll + u
            out = advance(2 * reach + row, levels, coefs)
            for h in range(2):
                solved32[h, pl.ds(row, STRIPS, stride=strip), :] = out[h]
        return levels, coefs

    lax.fori_loop(0, strip // unroll, turn, (levels, coefs))

    def pack(b, _):
        rows = pl.ds(pl.multiple_of(b * block, block), block)
        for h in range(2):
            solved[b, q * block:(q + 1) * block, h * 128:(h + 1) * 128] = solved32[h, rows, :].astype(BF16)
        return 0

    lax.fori_loop(0, N_CABLE, pack, 0)


def main_kernel(rows_all, frames, tension, step_index, owner, basis, singular,
                upper, inverse, rest, snaps,
                padded, halo, tens_halo, tens_rows, weights, solved32, solved, scaled, rows32, basis_out, basis_in,
                snaps_in, a, local1, total1, local2, half1, parts1, lines1, send1, recv1,
                half2, parts2, lines2, send2, recv2, halo_send, halo_recv, b_send, b_recv, s_send, s_recv):
    cable, seg = lax.axis_index("cable"), lax.axis_index("seg")
    nodes = frames.shape[0]
    strip = nodes // STRIPS
    block = nodes // N_CABLE
    positions = 2 * N_CABLE
    met = greet()

    pick = (lax.broadcasted_iota(jnp.int32, (positions, positions), 0) == owner[...]).astype(F32)
    pick_bf = pick.astype(BF16)
    unpick_bf = pick.T.astype(BF16)
    scaled[...] = (basis[...].astype(F32) * singular[...]).astype(BF16)

    def by_streamer(n, _):
        rows = scaled[pl.ds(pl.multiple_of(n * positions, positions), positions), :]
        moved = nn(pick_bf, rows)
        for h in range(2):
            rows32[h, pl.ds(n, positions, stride=block), :] = moved[:, h * 128:(h + 1) * 128]
        return 0

    lax.fori_loop(0, block, by_streamer, 0, unroll=4)
    for h in range(2):
        basis_out[:, :, h * 128:(h + 1) * 128] = rows32[h].astype(BF16).reshape(N_CABLE, 2 * block, 128)

    met()
    edges = Halo(frames, tension, halo, tens_halo, halo_send, halo_recv)
    edges.start()

    def exchange(d, out, into, send, recv, mine):
        peer = lax.rem(cable + d, N_CABLE)
        return pltpu.make_async_remote_copy(
            src_ref=out.at[peer], dst_ref=into.at[cable if mine else peer], send_sem=send.at[d],
            recv_sem=recv.at[cable if mine else peer], device_id=(peer, seg), device_id_type=MESH)

    each(1, N_CABLE, lambda d: exchange(d, basis_out, basis_in, b_send, b_recv, True).start())
    basis_in[cable] = basis_out[cable]

    local1[...] = tn(scaled[...], scaled[...])
    first = Reduce(local1, total1, half1, parts1, lines1, (send1, recv1))
    second = Reduce(local2, rest, half2, parts2, lines2, (send2, recv2))
    first.s0()
    for tile in range(4):
        padded[tile, EDGE:EDGE + nodes, :] = frames[:, tile * 128:(tile + 1) * 128].astype(F32)
    for q in range(2):
        for s in range(STRIPS):
            tens_rows[q, 8 + s:9 + s, :] = tension[q:q + 1, s * strip:(s + 1) * strip]
    edges.zero_ends()
    first.s1()
    edges.wait_recv()
    for tile in range(4):
        cols = slice(tile * 128, (tile + 1) * 128)
        padded[tile, 0:EDGE, :] = halo[0, :, cols].astype(F32)
        padded[tile, EDGE + nodes:, :] = halo[1, :, cols].astype(F32)
    make_weights(seg, tens_halo, tens_rows, weights, strip + 2 * SWEEPS)
    stiff = DRAG_RATE * (1.0 + step_index[...].astype(F32))
    scale = [jnp.broadcast_to(stiff[:, h * 128:(h + 1) * 128], (STRIPS, 128)) for h in range(2)]
    relax(0, scale, padded, weights, solved32, solved, strip, block)
    first.s2()
    relax(1, scale, padded, weights, solved32, solved, strip, block)
    first.s3()
    flat = solved[...].reshape(2 * nodes, SNAP)
    local2[K:, :] = tn(flat, flat)
    first.s4()
    first.s5()
    a[...] = total1[...] * (1.0 / rows_all)

    def cross():
        each(1, N_CABLE, lambda d: exchange(d, basis_out, basis_in, b_send, b_recv, False).wait_recv())
        local2[:K, :] = tn(solved[...].reshape(2 * nodes, SNAP), basis_in[...].reshape(2 * nodes, K))
        second.s0()

    def scatter():
        second.s1()
        each(1, N_CABLE, lambda d: exchange(d, solved, snaps_in, s_send, s_recv, True).start())
        snaps_in[cable] = solved[cable]

    factor_256(a, upper, inverse, (cross, scatter, second.s2))
    second.s3()
    each(1, N_CABLE, lambda d: exchange(d, solved, snaps_in, s_send, s_recv, False).wait_recv())

    for h in range(2):
        rows32[h] = snaps_in[:, :, h * 128:(h + 1) * 128].astype(F32).reshape(positions * block, 128)

    def by_position(n, _):
        rows = jnp.concatenate([rows32[h, pl.ds(n, positions, stride=block), :] for h in range(2)], axis=1)
        snaps[pl.ds(pl.multiple_of(n * positions, positions), positions), :] = (
            nn(unpick_bf, rows.astype(BF16)).astype(BF16))
        return 0

    lax.fori_loop(0, block, by_position, 0, unroll=4)
    second.s4()
    second.s5()

    first.drain()
    second.drain()
    edges.wait_send()
    each(1, N_CABLE, lambda d: exchange(d, basis_out, basis_in, b_send, b_recv, True).wait_send())
    each(1, N_CABLE, lambda d: exchange(d, solved, snaps_in, s_send, s_recv, True).wait_send())


def exchange_and_reduce(rows_all, frames, tension, step_index, owner_map, basis, singular):
    nodes = frames.shape[0]
    rows = basis.shape[0]
    block = nodes // N_CABLE
    steps = nodes // STRIPS + 2 * SWEEPS
    dma = pltpu.SemaphoreType.DMA
    square = jax.ShapeDtypeStruct((K, K), F32)
    return pl.pallas_call(
        lambda *refs: main_kernel(rows_all, *refs),
        out_shape=[square, square, jax.ShapeDtypeStruct((2 * K, K), F32), jax.ShapeDtypeStruct((rows, SNAP), BF16)],
        in_specs=[vmem_spec()] * 6,
        out_specs=[vmem_spec()] * 4,
        scratch_shapes=[
            VMEM((4, nodes + 2 * EDGE, 128), F32),
            VMEM((2, EDGE, 2 * SNAP), BF16),
            VMEM((2, 2, 128), F32),
            VMEM((2, 24, 128), F32),
            VMEM((2, 2, steps, STRIPS, 128), F32),
            VMEM((2, nodes, 128), F32),
            VMEM((N_CABLE, 2 * block, SNAP), BF16),
            VMEM((rows, K), BF16),
            VMEM((2, rows, 128), F32),
            VMEM((N_CABLE, 2 * block, K), BF16),
            VMEM((N_CABLE, 2 * block, K), BF16),
            VMEM((N_CABLE, 2 * block, SNAP), BF16),
            VMEM((K, K), F32),
            VMEM((K, K), F32),
            VMEM((K, K), F32),
            VMEM((2 * K, K), F32),
            *reduce_scratch(K), *reduce_scratch(2 * K),
            dma((4,)), dma((4,)), *[dma((N_CABLE,))] * 4,
        ],
        compiler_params=pltpu.CompilerParams(collective_id=0, has_side_effects=True, vmem_limit_bytes=48 * 2**20),
        name="relax_exchange_reduce",
    )(frames, tension, step_index, owner_map, basis, singular)


def rotate_kernel(rows_all, upper1, w1_ref, rest, basis, singular, snaps, factor, new_basis, a, inv2):
    scale = 1.0 / rows_all
    w1 = w1_ref[...]
    factor[:K, :K] = upper1[...]
    low = nt(rest[:K, :] * scale, w1, HI)
    factor[:K, K:] = low.T
    factor[K:, :K] = jnp.zeros((K, K), F32)
    a[...] = rest[K:, :] * scale - nt(low, low, HI)
    t = nn(low, w1, HI)
    factor_256(a, factor.at[K:, K:], inv2)
    w2 = inv2[...]
    cross = (-nn(w2, t, HI)).astype(BF16)
    w1b, w2b = w1.astype(BF16), w2.astype(BF16)
    scaled = (basis[...].astype(F32) * singular[...]).astype(BF16)
    new_basis[:, :K] = nt(scaled, w1b).astype(BF16)
    new_basis[:, K:] = (nt(scaled, cross) + nt(snaps[...], w2b)).astype(BF16)


def factor_and_rotate(rows_all, upper, inverse, rest, basis, singular, snaps):
    rows, width = basis.shape[0], 2 * K
    return pl.pallas_call(
        lambda *refs: rotate_kernel(rows_all, *refs),
        out_shape=[jax.ShapeDtypeStruct((width, width), F32), jax.ShapeDtypeStruct((rows, width), BF16)],
        in_specs=[vmem_spec()] * 6,
        out_specs=[vmem_spec()] * 2,
        scratch_shapes=[VMEM((K, K), F32)] * 2,
        compiler_params=pltpu.CompilerParams(vmem_limit_bytes=40 * 2**20),
        name="factor_rotate",
    )(upper, inverse, rest, basis, singular, snaps)


def body(frames, tension, step_index, owner_map, old_basis, singular):
    nodes = frames.shape[0]
    basis = old_basis.reshape(-1, K)
    gain = singular[None, :]
    rows_all = basis.shape[0] * lax.axis_size("cable") * lax.axis_size("seg")
    upper, inverse, rest, snaps = exchange_and_reduce(
        rows_all, frames.reshape(nodes, 2 * SNAP), tension.T, step_index[None, :], owner_map[None, :], basis, gain)
    factor, rotated = factor_and_rotate(rows_all, upper, inverse, rest, basis, gain, snaps)
    return factor, rotated.reshape(old_basis.shape[:3] + (2 * K,))


def solution(mesh):
    return jax.shard_map(
        body,
        mesh=mesh,
        in_specs=(P("seg", "cable", None), P("seg", "cable"), P(), P(), P("seg", "cable", None, None), P()),
        out_specs=(P(), P("seg", "cable", None, None)),
        check_vma=False,
    )
```

time: 451 us -> 91.4 us (0.20); the launches traced: 443 us -> 91.2 us
  other arithmetic: 170 us -> 0 us
  waiting for transfers between devices: 160 us -> 0 us
  Pallas kernels: 0 us -> 89 us
  starting transfers between devices: 61.3 us -> 0 us
  local copies, waits for them, and re-layouts: 19.5 us -> 1.55 us
  between operations: 18 us -> 0.73 us
  matrix products: 14.6 us -> 0 us
    psum x1 -> x0, waiting for transfers between devices: 144 us -> none  [body(): gram_sum = lax.psum(gram_local, ('cable', 'seg'))]
    another operation x17 -> x0, other arithmetic: 120 us -> none  [the longest x14 78.7 us: body(): lower_chol = jnp.linalg.cholesky(gram_sum)]
    pallas_call x0 -> x2, Pallas kernels: none -> 89 us  [the longest x1 75.5 us: exchange_and_reduce(): pl.pallas_call(lambda *refs: main_kernel(rows_all, *refs), out_shape=[squ...]
    ppermute x14 -> x0, starting transfers between devices: 52.4 us -> none  [the longest x7 37.6 us: padded_2(): lax.ppermute(lax.slice_in_dim(block, block.shape[dim] - width, None, axis...]
    div x7 -> x0, other arithmetic: 34.4 us -> none  [the longest x5 32.8 us: body(): (source + stiffness * (right_weight * padded[2:] + left_weight * padded[:...]
    another operation x17 -> x0, local copies, waits for them, and re-layouts: 14.1 us -> none
    all_to_all x1 -> x0, waiting for transfers between devices: 13.4 us -> none  [body(): lax.all_to_all(solved, 'cable', split_axis=0, concat_axis=1, tiled=True)]
    convert_element_type x5 -> x0, other arithmetic: 12.9 us -> none  [the longest x1 7.08 us: body(): solved = current.astype(jnp.bfloat16)]
  transfers between devices with their start and end apart: 16 -> 0, of which waited for: 6 -> 0; matrix products, arithmetic and copies ran while one was open for 2% -> 0% of each run, Pallas kernels for 0% -> 0%
where the time goes in v2:
time: 91.4 us; the launch traced here: 91.2 us
  Pallas kernels  89 us (97%)
  local copies, waits for them, and re-layouts  1.55 us (2%)
    pallas_call x1, Pallas kernels, exchange_and_reduce(): pl.pallas_call(lambda *refs: main_kernel(rows_all, *refs), out_shape=[squ...  75.5 us
    pallas_call x1, Pallas kernels, factor_and_rotate(): pl.pallas_call(lambda *refs: rotate_kernel(rows_all, *refs), out_shape=[j...  13.4 us

profile of v2, /device:TPU:1, one launch (start us, length us, event | category | flops | bytes accessed | tf_op | source)
XLA Modules:
  0.0 91.2 jit_solution(10466420113161871350)
XLA Ops:
  0.6 0.0 copy-start.2
  0.6 0.0 copy-start
  0.7 0.0 copy-start.4
  0.7 0.0 copy-start.3
  0.7 0.0 copy-start.1
  0.7 1.5 %copy.8 = bf16[128,8,2,256]{3,1,2,0:T(8,128)(2,1)S(1)} copy(bf16[128,8,2,256]{3,2,1,0:T(2,128)(2,1)} %bitcast.16) | data formatting | bytes 2097152
  2.2 0.0 copy-done.2
  2.2 0.0 copy-done
  2.2 0.0 copy-done.4
  2.2 0.0 copy-done.3
  2.3 0.0 copy-done.1
  2.3 75.5 %relax_exchange_reduce.1 = (f32[256,256]{1,0:T(8,128)S(1)}, f32[256,256]{1,0:T(8,128)S(1)}, f32[512,256]{1,0:T(8,128)S(1)}, bf16[2048,256]{1,0:T(8,128)(2,1)S(1)}) custom-call(bf16[1024,512]{1,0:T(8,128)(2,1)S(1)} %bitcast.10, f32[2,1024]{1,0:T(2,128)S(1)} %bitcast.11, s32[1,256]{1,0:T(1,128)S(1)} %bitcast.14, s32[1,64]{1,0:T(1,128)S(1)} %bitcast.15, ...), custom_call_target="tpu_custom_call" | custom-call | tf_op jit(solution)/shard_map/relax_exchange_reduce/pallas_call | solution.py:481
  77.8 13.4 %factor_rotate.1 = (f32[512,512]{1,0:T(8,128)}, bf16[2048,512]{1,0:T(8,128)(2,1)}) custom-call(f32[256,256]{1,0:T(8,128)S(1)} %get-tuple-element.8.refs_0_, f32[256,256]{1,0:T(8,128)S(1)} %get-tuple-element.9.refs_1_, f32[512,256]{1,0:T(8,128)S(1)} %get-tuple-element.10.refs_2_, bf16[2048,256]{1,0:T(8,128)(2,1)S(1)} %bitcast.9, f32[1,256]{1,0:T(1,128)S(1)} %bitcast.13, ...), custom_call_target="tpu_custom_call" | custom-call | tf_op jit(solution)/shard_map/factor_rotate/pallas_call | solution.py:531
Async XLA Ops:
  0.6 1.6 %copy-start.2 = (f32[256]{0:T(256)S(1)}, f32[256]{0:T(256)}, u32[]{:S(2)}) copy-start(f32[256]{0:T(256)} %param.11) | copy-start | bytes 3076
  0.6 1.6 %copy-start = (bf16[1,32,64,256]{3,2,1,0:T(8,128)(2,1)S(1)}, bf16[1,32,64,256]{3,2,1,0:T(8,128)(2,1)}, u32[]{:S(2)}) copy-start(bf16[1,32,64,256]{3,2,1,0:T(8,128)(2,1)} %param.10) | copy-start | bytes 3145732
  0.7 1.6 %copy-start.4 = (s32[64]{0:T(128)S(1)}, s32[64]{0:T(128)}, u32[]{:S(2)}) copy-start(s32[64]{0:T(128)} %param.9) | copy-start | bytes 772
  0.7 1.6 %copy-start.3 = (s32[256]{0:T(256)S(1)}, s32[256]{0:T(256)}, u32[]{:S(2)}) copy-start(s32[256]{0:T(256)} %param.8) | copy-start | bytes 3076
  0.7 1.6 %copy-start.1 = (f32[1024,2]{0,1:T(2,128)S(1)}, f32[1024,2]{0,1:T(2,128)}, u32[]{:S(2)}) copy-start(f32[1024,2]{0,1:T(2,128)} %param.7) | copy-start | bytes 24580

commit v3 on v2

--- a/solution.py
+++ b/solution.py
@@ -165,13 +165,15 @@
             pltpu.SemaphoreType.DMA((48,)), pltpu.SemaphoreType.DMA((48,))]
 
 
-def factor_128(a, upper, inverse):
+def factor_128(a, upper, inverse, hooks=None, base=0):
     size, n = 8, 16
     rows = lax.broadcasted_iota(jnp.int32, (size, 128), 0)
     lanes = lax.broadcasted_iota(jnp.int32, (size, 128), 1)
     depth = lax.broadcasted_iota(jnp.int32, (n, size, 128), 0)
     q = jnp.where(lanes[None] == rows[None] + size * depth, 1.0, 0.0).astype(F32)
     for kb in range(n):
+        if hooks is not None and base + kb in hooks:
+            hooks[base + kb]()
         at = size * kb
         own, own_q = a[0], q[0]
         a, q = a[1:], q[1:]
@@ -212,11 +214,9 @@
         inverse[at:at + size, :] = jnp.where(lanes <= rows + at, wt, 0.0)
 
 
-def factor_256(a, upper, inverse, between=None):
+def factor_256(a, upper, inverse, hooks=None):
     h = 128
-    factor_128(a[:h, :h].reshape(16, 8, h), upper.at[:h, :h], inverse.at[:h, :h])
-    if between is not None:
-        between[0]()
+    factor_128(a[:h, :h].reshape(16, 8, h), upper.at[:h, :h], inverse.at[:h, :h], hooks)
     w1 = inverse[:h, :h]
     low = nt(a[h:, :h], w1, HI)
     upper[:h, h:] = low.T
@@ -224,11 +224,7 @@
     inverse[:h, h:] = jnp.zeros((h, h), F32)
     a[h:, h:] = a[h:, h:] - nt(low, low, HI)
     t = nn(low, w1, HI)
-    if between is not None:
-        between[1]()
-    factor_128(a[h:, h:].reshape(16, 8, h), upper.at[h:, h:], inverse.at[h:, h:])
-    if between is not None:
-        between[2]()
+    factor_128(a[h:, h:].reshape(16, 8, h), upper.at[h:, h:], inverse.at[h:, h:], hooks, 16)
     inverse[h:, :h] = -nn(inverse[h:, h:], t, HI)
 
 
@@ -239,11 +235,11 @@
 
     def copies(self, side):
         frames, tension, halo, tens_halo, send, recv = self.refs
-        nodes = frames.shape[0]
+        nodes = frames.shape[0] // 4
         peer = self.seg + 1 if side == 0 else self.seg - 1
         return [
             pltpu.make_async_remote_copy(
-                src_ref=frames.at[pl.ds(nodes - EDGE if side == 0 else 0, EDGE), :], dst_ref=halo.at[side],
+                src_ref=frames.at[pl.ds(4 * (nodes - EDGE) if side == 0 else 0, 4 * EDGE), :], dst_ref=halo.at[side],
                 send_sem=send.at[side], recv_sem=recv.at[side],
                 device_id=(self.cable, peer), device_id_type=MESH),
             pltpu.make_async_remote_copy(
@@ -323,7 +319,7 @@
         total = lw + rw
         out = []
         for h in range(2):
-            value = padded[2 * q + h, pl.ds(EDGE - reach + step, STRIPS, stride=strip), :]
+            value = padded[pl.ds(4 * (EDGE - reach + step) + 2 * h + q, STRIPS, stride=4 * strip), :]
             inv = 1.0 / (1.0 + scale[h] * total)
             si = scale[h] * inv
             coefs[h].append((si * lw, si * rw, value * inv))
@@ -368,21 +364,35 @@
 
 
 def main_kernel(rows_all, frames, tension, step_index, owner, basis, singular,
-                upper, inverse, rest, snaps,
+                factor, w1_out, w2_out, cross_out, snaps,
                 padded, halo, tens_halo, tens_rows, weights, solved32, solved, scaled, rows32, basis_out, basis_in,
-                snaps_in, a, local1, total1, local2, half1, parts1, lines1, send1, recv1,
+                snaps_in, a, inverse1, inverse2, local1, total1, local2, total2, half1, parts1, lines1, send1, recv1,
                 half2, parts2, lines2, send2, recv2, halo_send, halo_recv, b_send, b_recv, s_send, s_recv):
     cable, seg = lax.axis_index("cable"), lax.axis_index("seg")
-    nodes = frames.shape[0]
+    nodes = frames.shape[0] // 4
     strip = nodes // STRIPS
     block = nodes // N_CABLE
     positions = 2 * N_CABLE
+    scale_all = 1.0 / rows_all
     met = greet()
+
+    scaled[...] = (basis[...].astype(F32) * singular[...]).astype(BF16)
+    local1[...] = tn(scaled[...], scaled[...])
+    padded[4 * EDGE:4 * (EDGE + nodes), :] = frames[...].astype(F32)
+    for q in range(2):
+        for s in range(STRIPS):
+            tens_rows[q, 8 + s:9 + s, :] = tension[q:q + 1, s * strip:(s + 1) * strip]
+    first = Reduce(local1, total1, half1, parts1, lines1, (send1, recv1))
+    second = Reduce(local2, total2, half2, parts2, lines2, (send2, recv2))
+    edges = Halo(frames, tension, halo, tens_halo, halo_send, halo_recv)
+    edges.zero_ends()
+    met()
+    first.s0()
+    edges.start()
 
     pick = (lax.broadcasted_iota(jnp.int32, (positions, positions), 0) == owner[...]).astype(F32)
     pick_bf = pick.astype(BF16)
     unpick_bf = pick.T.astype(BF16)
-    scaled[...] = (basis[...].astype(F32) * singular[...]).astype(BF16)
 
     def by_streamer(n, _):
         rows = scaled[pl.ds(pl.multiple_of(n * positions, positions), positions), :]
@@ -394,10 +404,7 @@
     lax.fori_loop(0, block, by_streamer, 0, unroll=4)
     for h in range(2):
         basis_out[:, :, h * 128:(h + 1) * 128] = rows32[h].astype(BF16).reshape(N_CABLE, 2 * block, 128)
-
-    met()
-    edges = Halo(frames, tension, halo, tens_halo, halo_send, halo_recv)
-    edges.start()
+    first.s1()
 
     def exchange(d, out, into, send, recv, mine):
         peer = lax.rem(cable + d, N_CABLE)
@@ -405,51 +412,55 @@
             src_ref=out.at[peer], dst_ref=into.at[cable if mine else peer], send_sem=send.at[d],
             recv_sem=recv.at[cable if mine else peer], device_id=(peer, seg), device_id_type=MESH)
 
-    each(1, N_CABLE, lambda d: exchange(d, basis_out, basis_in, b_send, b_recv, True).start())
+    def basis_trip(d, mine):
+        return exchange(d, basis_out, basis_in, b_send, b_recv, mine)
+
+    def snaps_trip(d, mine):
+        return exchange(d, solved, snaps_in, s_send, s_recv, mine)
+
+    each(1, N_CABLE, lambda d: basis_trip(d, True).start())
     basis_in[cable] = basis_out[cable]
 
-    local1[...] = tn(scaled[...], scaled[...])
-    first = Reduce(local1, total1, half1, parts1, lines1, (send1, recv1))
-    second = Reduce(local2, rest, half2, parts2, lines2, (send2, recv2))
-    first.s0()
-    for tile in range(4):
-        padded[tile, EDGE:EDGE + nodes, :] = frames[:, tile * 128:(tile + 1) * 128].astype(F32)
-    for q in range(2):
-        for s in range(STRIPS):
-            tens_rows[q, 8 + s:9 + s, :] = tension[q:q + 1, s * strip:(s + 1) * strip]
-    edges.zero_ends()
-    first.s1()
     edges.wait_recv()
-    for tile in range(4):
-        cols = slice(tile * 128, (tile + 1) * 128)
-        padded[tile, 0:EDGE, :] = halo[0, :, cols].astype(F32)
-        padded[tile, EDGE + nodes:, :] = halo[1, :, cols].astype(F32)
+    padded[0:4 * EDGE, :] = halo[0].astype(F32)
+    padded[4 * (EDGE + nodes):, :] = halo[1].astype(F32)
     make_weights(seg, tens_halo, tens_rows, weights, strip + 2 * SWEEPS)
     stiff = DRAG_RATE * (1.0 + step_index[...].astype(F32))
     scale = [jnp.broadcast_to(stiff[:, h * 128:(h + 1) * 128], (STRIPS, 128)) for h in range(2)]
     relax(0, scale, padded, weights, solved32, solved, strip, block)
     first.s2()
     relax(1, scale, padded, weights, solved32, solved, strip, block)
-    first.s3()
     flat = solved[...].reshape(2 * nodes, SNAP)
     local2[K:, :] = tn(flat, flat)
+    first.s3()
+    each(1, N_CABLE, lambda d: basis_trip(d, False).wait_recv())
+    local2[:K, :] = tn(flat, basis_in[...].reshape(2 * nodes, K))
+    second.s0()
+    second.s1()
     first.s4()
     first.s5()
-    a[...] = total1[...] * (1.0 / rows_all)
-
-    def cross():
-        each(1, N_CABLE, lambda d: exchange(d, basis_out, basis_in, b_send, b_recv, False).wait_recv())
-        local2[:K, :] = tn(solved[...].reshape(2 * nodes, SNAP), basis_in[...].reshape(2 * nodes, K))
-        second.s0()
-
-    def scatter():
-        second.s1()
-        each(1, N_CABLE, lambda d: exchange(d, solved, snaps_in, s_send, s_recv, True).start())
+    a[...] = total1[...] * scale_all
+
+    def send_snaps():
+        second.s3()
+        each(1, N_CABLE, lambda d: snaps_trip(d, True).start())
         snaps_in[cable] = solved[cable]
 
-    factor_256(a, upper, inverse, (cross, scatter, second.s2))
-    second.s3()
-    each(1, N_CABLE, lambda d: exchange(d, solved, snaps_in, s_send, s_recv, False).wait_recv())
+    factor_256(a, factor.at[:K, :K], inverse1, {16: second.s2, 28: send_snaps})
+    w1 = inverse1[...]
+    w1_out[...] = w1.astype(BF16)
+    factor[K:, :K] = jnp.zeros((K, K), F32)
+    second.s4()
+    second.s5()
+    low = nt(total2[:K, :] * scale_all, w1, HI)
+    factor[:K, K:] = low.T
+    a[...] = total2[K:, :] * scale_all - nt(low, low, HI)
+    t = nn(low, w1, HI)
+    factor_256(a, factor.at[K:, K:], inverse2)
+    w2 = inverse2[...]
+    w2_out[...] = w2.astype(BF16)
+    cross_out[...] = (-nn(w2, t, HI)).astype(BF16)
+    each(1, N_CABLE, lambda d: snaps_trip(d, False).wait_recv())
 
     for h in range(2):
         rows32[h] = snaps_in[:, :, h * 128:(h + 1) * 128].astype(F32).reshape(positions * block, 128)
@@ -461,31 +472,29 @@
         return 0
 
     lax.fori_loop(0, block, by_position, 0, unroll=4)
-    second.s4()
-    second.s5()
-
     first.drain()
     second.drain()
     edges.wait_send()
-    each(1, N_CABLE, lambda d: exchange(d, basis_out, basis_in, b_send, b_recv, True).wait_send())
-    each(1, N_CABLE, lambda d: exchange(d, solved, snaps_in, s_send, s_recv, True).wait_send())
-
-
-def exchange_and_reduce(rows_all, frames, tension, step_index, owner_map, basis, singular):
-    nodes = frames.shape[0]
+    each(1, N_CABLE, lambda d: basis_trip(d, True).wait_send())
+    each(1, N_CABLE, lambda d: snaps_trip(d, True).wait_send())
+
+
+def exchange_and_factor(rows_all, frames, tension, step_index, owner_map, basis, singular):
+    nodes = frames.shape[0] // 4
     rows = basis.shape[0]
     block = nodes // N_CABLE
     steps = nodes // STRIPS + 2 * SWEEPS
     dma = pltpu.SemaphoreType.DMA
-    square = jax.ShapeDtypeStruct((K, K), F32)
+    square = jax.ShapeDtypeStruct((K, K), BF16)
     return pl.pallas_call(
         lambda *refs: main_kernel(rows_all, *refs),
-        out_shape=[square, square, jax.ShapeDtypeStruct((2 * K, K), F32), jax.ShapeDtypeStruct((rows, SNAP), BF16)],
+        out_shape=[jax.ShapeDtypeStruct((2 * K, 2 * K), F32), square, square, square,
+                   jax.ShapeDtypeStruct((rows, SNAP), BF16)],
         in_specs=[vmem_spec()] * 6,
-        out_specs=[vmem_spec()] * 4,
+        out_specs=[vmem_spec()] * 5,
         scratch_shapes=[
-            VMEM((4, nodes + 2 * EDGE, 128), F32),
-            VMEM((2, EDGE, 2 * SNAP), BF16),
+            VMEM((4 * (nodes + 2 * EDGE), 128), F32),
+            VMEM((2, 4 * EDGE, 128), BF16),
             VMEM((2, 2, 128), F32),
             VMEM((2, 24, 128), F32),
             VMEM((2, 2, steps, STRIPS, 128), F32),
@@ -499,44 +508,39 @@
             VMEM((K, K), F32),
             VMEM((K, K), F32),
             VMEM((K, K), F32),
+            VMEM((K, K), F32),
+            VMEM((K, K), F32),
+            VMEM((2 * K, K), F32),
             VMEM((2 * K, K), F32),
             *reduce_scratch(K), *reduce_scratch(2 * K),
             dma((4,)), dma((4,)), *[dma((N_CABLE,))] * 4,
         ],
         compiler_params=pltpu.CompilerParams(collective_id=0, has_side_effects=True, vmem_limit_bytes=48 * 2**20),
-        name="relax_exchange_reduce",
+        name="relax_exchange_factor",
     )(frames, tension, step_index, owner_map, basis, singular)
 
 
-def rotate_kernel(rows_all, upper1, w1_ref, rest, basis, singular, snaps, factor, new_basis, a, inv2):
-    scale = 1.0 / rows_all
-    w1 = w1_ref[...]
-    factor[:K, :K] = upper1[...]
-    low = nt(rest[:K, :] * scale, w1, HI)
-    factor[:K, K:] = low.T
-    factor[K:, :K] = jnp.zeros((K, K), F32)
-    a[...] = rest[K:, :] * scale - nt(low, low, HI)
-    t = nn(low, w1, HI)
-    factor_256(a, factor.at[K:, K:], inv2)
-    w2 = inv2[...]
-    cross = (-nn(w2, t, HI)).astype(BF16)
-    w1b, w2b = w1.astype(BF16), w2.astype(BF16)
+def rotate_kernel(factor_in, w1, w2, cross, basis, singular, snaps, factor, new_basis, sem):
+    copy = pltpu.make_async_copy(factor_in, factor, sem)
+    copy.start()
     scaled = (basis[...].astype(F32) * singular[...]).astype(BF16)
-    new_basis[:, :K] = nt(scaled, w1b).astype(BF16)
-    new_basis[:, K:] = (nt(scaled, cross) + nt(snaps[...], w2b)).astype(BF16)
-
-
-def factor_and_rotate(rows_all, upper, inverse, rest, basis, singular, snaps):
+    new_basis[:, :K] = nt(scaled, w1[...]).astype(BF16)
+    new_basis[:, K:] = (nt(scaled, cross[...]) + nt(snaps[...], w2[...])).astype(BF16)
+    copy.wait()
+
+
+def rotate(factor, w1, w2, cross, basis, singular, snaps):
     rows, width = basis.shape[0], 2 * K
+    anywhere = pl.BlockSpec(memory_space=pl.ANY)
     return pl.pallas_call(
-        lambda *refs: rotate_kernel(rows_all, *refs),
+        rotate_kernel,
         out_shape=[jax.ShapeDtypeStruct((width, width), F32), jax.ShapeDtypeStruct((rows, width), BF16)],
-        in_specs=[vmem_spec()] * 6,
-        out_specs=[vmem_spec()] * 2,
-        scratch_shapes=[VMEM((K, K), F32)] * 2,
+        in_specs=[anywhere] + [vmem_spec()] * 6,
+        out_specs=[anywhere, vmem_spec()],
+        scratch_shapes=[pltpu.SemaphoreType.DMA],
         compiler_params=pltpu.CompilerParams(vmem_limit_bytes=40 * 2**20),
-        name="factor_rotate",
-    )(upper, inverse, rest, basis, singular, snaps)
+        name="rotate",
+    )(factor, w1, w2, cross, basis, singular, snaps)
 
 
 def body(frames, tension, step_index, owner_map, old_basis, singular):
@@ -544,9 +548,10 @@
     basis = old_basis.reshape(-1, K)
     gain = singular[None, :]
     rows_all = basis.shape[0] * lax.axis_size("cable") * lax.axis_size("seg")
-    upper, inverse, rest, snaps = exchange_and_reduce(
-        rows_all, frames.reshape(nodes, 2 * SNAP), tension.T, step_index[None, :], owner_map[None, :], basis, gain)
-    factor, rotated = factor_and_rotate(rows_all, upper, inverse, rest, basis, gain, snaps)
+    lines = frames.reshape(nodes, 2, 2, 128).transpose(0, 2, 1, 3).reshape(4 * nodes, 128)
+    factor, w1, w2, cross, snaps = exchange_and_factor(
+        rows_all, lines, tension.T, step_index[None, :], owner_map[None, :], basis, gain)
+    factor, rotated = rotate(factor, w1, w2, cross, basis, gain, snaps)
     return factor, rotated.reshape(old_basis.shape[:3] + (2 * K,))
 
 

time: 91.4 us -> 90.9 us (level)
  the two profiles are of different devices: /device:TPU:1 before, /device:TPU:3 now
where the time goes in v3:
time: 90.9 us; the launch traced here: 90.6 us
  Pallas kernels  84.6 us (93%)
  local copies, waits for them, and re-layouts  5.15 us (6%)
    pallas_call x1, Pallas kernels, exchange_and_factor(): pl.pallas_call(lambda *refs: main_kernel(rows_all, *refs), out_shape=[jax...  82.2 us
    unnamed x12, local copies, waits for them, and re-layouts  5.15 us
    pallas_call x1, Pallas kernels, rotate(): pl.pallas_call(rotate_kernel, out_shape=[jax.ShapeDtypeStruct((width, wid...  2.4 us

profile of v3, /device:TPU:3, one launch (start us, length us, event | category | flops | bytes accessed | tf_op | source)
XLA Modules:
  0.0 90.6 jit_solution(15697383113858816739)
XLA Ops:
  0.6 0.0 copy-start
  0.6 1.2 %copy-done = bf16[1,32,64,256]{3,2,1,0:T(8,128)(2,1)S(1)} copy-done((bf16[1,32,64,256]{3,2,1,0:T(8,128)(2,1)S(1)}, bf16[1,32,64,256]{3,2,1,0:T(8,128)(2,1)}, u32[]{:S(2)}) %copy-start) | copy-done | bytes 1048600
  1.9 0.0 copy-start.1
  1.9 1.2 %copy-done.1 = bf16[1024,2,256]{2,1,0:T(2,128)(2,1)S(1)} copy-done((bf16[1024,2,256]{2,1,0:T(2,128)(2,1)S(1)}, bf16[1024,2,256]{2,1,0:T(2,128)(2,1)}, u32[]{:S(2)}) %copy-start.1) | copy-done | bytes 1048600
  3.1 0.0 copy-start.2
  3.1 0.7 copy-done.2
  3.8 0.0 copy-start.3
  3.8 0.7 copy-done.3
  4.5 0.0 copy-start.4
  4.5 0.7 copy-done.4
  5.1 0.0 copy-start.5
  5.1 0.7 copy-done.5
  5.8 82.2 %relax_exchange_factor.1 = (f32[512,512]{1,0:T(8,128)S(1)}, bf16[256,256]{1,0:T(8,128)(2,1)S(1)}, bf16[256,256]{1,0:T(8,128)(2,1)S(1)}, bf16[256,256]{1,0:T(8,128)(2,1)S(1)}, bf16[2048,256]{1,0:T(8,128)(2,1)S(1)}) custom-call(bf16[4096,128]{1,0:T(8,128)(2,1)S(1)} %bitcast.13, f32[2,1024]{1,0:T(2,128)S(1)} %bitcast.14, s32[1,256]{1,0:T(1,128)S(1)} %bitcast.17, ...), custom_call_target="tpu_custom_call" | custom-call | tf_op jit(solution)/shard_map/relax_exchange_factor/pallas_call | solution.py:489
  88.0 2.4 %rotate.1 = (f32[512,512]{1,0:T(8,128)}, bf16[2048,512]{1,0:T(8,128)(2,1)}) custom-call(f32[512,512]{1,0:T(8,128)S(1)} %get-tuple-element.9.factor_in, bf16[256,256]{1,0:T(8,128)(2,1)S(1)} %get-tuple-element.10.w1, bf16[256,256]{1,0:T(8,128)(2,1)S(1)} %get-tuple-element.11.w2, bf16[256,256]{1,0:T(8,128)(2,1)S(1)} %get-tuple-element.12.cross, ...), custom_call_target="tpu_custom_call" | custom-call | tf_op jit(solution)/shard_map/rotate/pallas_call | solution.py:535
Async XLA Ops:
  0.6 1.2 %copy-start = (bf16[1,32,64,256]{3,2,1,0:T(8,128)(2,1)S(1)}, bf16[1,32,64,256]{3,2,1,0:T(8,128)(2,1)}, u32[]{:S(2)}) copy-start(bf16[1,32,64,256]{3,2,1,0:T(8,128)(2,1)} %param.10) | copy-start | bytes 3145732
  1.9 1.2 %copy-start.1 = (bf16[1024,2,256]{2,1,0:T(2,128)(2,1)S(1)}, bf16[1024,2,256]{2,1,0:T(2,128)(2,1)}, u32[]{:S(2)}) copy-start(bf16[1024,2,256]{2,1,0:T(2,128)(2,1)} %param.6) | copy-start | bytes 3145732
  3.1 0.7 copy-start.2
  3.8 0.7 copy-start.3
  4.5 0.7 copy-start.4
  5.1 0.7 copy-start.5

commit v4 on v3

--- a/solution.py
+++ b/solution.py
@@ -363,33 +363,27 @@
     lax.fori_loop(0, N_CABLE, pack, 0)
 
 
-def main_kernel(rows_all, frames, tension, step_index, owner, basis, singular,
+def main_kernel(rows_all, frames_in, tension_in, step_in, owner_in, basis_hbm, singular_in,
                 factor, w1_out, w2_out, cross_out, snaps,
-                padded, halo, tens_halo, tens_rows, weights, solved32, solved, scaled, rows32, basis_out, basis_in,
+                frames, tension, step_index, owner, basis, singular, load_sem, padded, halo, tens_halo, tens_rows, weights, solved32, solved, scaled, rows32, basis_out, basis_in,
                 snaps_in, a, inverse1, inverse2, local1, total1, local2, total2, half1, parts1, lines1, send1, recv1,
                 half2, parts2, lines2, send2, recv2, halo_send, halo_recv, b_send, b_recv, s_send, s_recv):
     cable, seg = lax.axis_index("cable"), lax.axis_index("seg")
-    nodes = frames.shape[0] // 4
+    nodes = frames_in.shape[0] // 4
     strip = nodes // STRIPS
     block = nodes // N_CABLE
     positions = 2 * N_CABLE
     scale_all = 1.0 / rows_all
     met = greet()
-
+    loads = [pltpu.make_async_copy(src, dst, load_sem.at[i]) for i, (src, dst) in enumerate((
+        (basis_hbm, basis), (singular_in, singular), (owner_in, owner), (frames_in, frames), (tension_in, tension),
+        (step_in, step_index)))]
+    for load in loads:
+        load.start()
+
+    for load in loads[:3]:
+        load.wait()
     scaled[...] = (basis[...].astype(F32) * singular[...]).astype(BF16)
-    local1[...] = tn(scaled[...], scaled[...])
-    padded[4 * EDGE:4 * (EDGE + nodes), :] = frames[...].astype(F32)
-    for q in range(2):
-        for s in range(STRIPS):
-            tens_rows[q, 8 + s:9 + s, :] = tension[q:q + 1, s * strip:(s + 1) * strip]
-    first = Reduce(local1, total1, half1, parts1, lines1, (send1, recv1))
-    second = Reduce(local2, total2, half2, parts2, lines2, (send2, recv2))
-    edges = Halo(frames, tension, halo, tens_halo, halo_send, halo_recv)
-    edges.zero_ends()
-    met()
-    first.s0()
-    edges.start()
-
     pick = (lax.broadcasted_iota(jnp.int32, (positions, positions), 0) == owner[...]).astype(F32)
     pick_bf = pick.astype(BF16)
     unpick_bf = pick.T.astype(BF16)
@@ -404,49 +398,72 @@
     lax.fori_loop(0, block, by_streamer, 0, unroll=4)
     for h in range(2):
         basis_out[:, :, h * 128:(h + 1) * 128] = rows32[h].astype(BF16).reshape(N_CABLE, 2 * block, 128)
+    for load in loads[3:]:
+        load.wait()
+    first = Reduce(local1, total1, half1, parts1, lines1, (send1, recv1))
+    second = Reduce(local2, total2, half2, parts2, lines2, (send2, recv2))
+    edges = Halo(frames, tension, halo, tens_halo, halo_send, halo_recv)
+    edges.zero_ends()
+
+    def exchange(d, out, into, q, send, recv, mine):
+        peer = lax.rem(cable + d, N_CABLE)
+        rows = pl.ds(q * block, block)
+        return pltpu.make_async_remote_copy(
+            src_ref=out.at[peer, rows, :], dst_ref=into.at[cable if mine else peer, rows, :], send_sem=send.at[q, d],
+            recv_sem=recv.at[q, cable if mine else peer], device_id=(peer, seg), device_id_type=MESH)
+
+    def basis_trip(d, mine):
+        return exchange(d, basis_out, basis_in, 0, b_send, b_recv, mine)
+
+    def snaps_trip(q, d, mine):
+        return exchange(d, solved, snaps_in, q, s_send, s_recv, mine)
+
+    def send_snaps(q):
+        each(1, N_CABLE, lambda d: snaps_trip(q, d, True).start())
+        snaps_in[cable, q * block:(q + 1) * block, :] = solved[cable, q * block:(q + 1) * block, :]
+
+    def half(ref, q):
+        return ref[:, q * block:(q + 1) * block, :].reshape(nodes, K)
+
+    met()
+    edges.start()
+    each(1, N_CABLE, lambda d: basis_trip(d, True).start())
+    local1[...] = tn(scaled[...], scaled[...])
+    first.s0()
+    basis_in[cable, 0:block, :] = basis_out[cable, 0:block, :]
+    padded[4 * EDGE:4 * (EDGE + nodes), :] = frames[...].astype(F32)
+    for q in range(2):
+        for s in range(STRIPS):
+            tens_rows[q, 8 + s:9 + s, :] = tension[q:q + 1, s * strip:(s + 1) * strip]
     first.s1()
-
-    def exchange(d, out, into, send, recv, mine):
-        peer = lax.rem(cable + d, N_CABLE)
-        return pltpu.make_async_remote_copy(
-            src_ref=out.at[peer], dst_ref=into.at[cable if mine else peer], send_sem=send.at[d],
-            recv_sem=recv.at[cable if mine else peer], device_id=(peer, seg), device_id_type=MESH)
-
-    def basis_trip(d, mine):
-        return exchange(d, basis_out, basis_in, b_send, b_recv, mine)
-
-    def snaps_trip(d, mine):
-        return exchange(d, solved, snaps_in, s_send, s_recv, mine)
-
-    each(1, N_CABLE, lambda d: basis_trip(d, True).start())
-    basis_in[cable] = basis_out[cable]
-
     edges.wait_recv()
     padded[0:4 * EDGE, :] = halo[0].astype(F32)
     padded[4 * (EDGE + nodes):, :] = halo[1].astype(F32)
     make_weights(seg, tens_halo, tens_rows, weights, strip + 2 * SWEEPS)
     stiff = DRAG_RATE * (1.0 + step_index[...].astype(F32))
     scale = [jnp.broadcast_to(stiff[:, h * 128:(h + 1) * 128], (STRIPS, 128)) for h in range(2)]
+    relax(1, scale, padded, weights, solved32, solved, strip, block)
+    send_snaps(1)
+    first.s2()
     relax(0, scale, padded, weights, solved32, solved, strip, block)
-    first.s2()
-    relax(1, scale, padded, weights, solved32, solved, strip, block)
     flat = solved[...].reshape(2 * nodes, SNAP)
     local2[K:, :] = tn(flat, flat)
     first.s3()
     each(1, N_CABLE, lambda d: basis_trip(d, False).wait_recv())
-    local2[:K, :] = tn(flat, basis_in[...].reshape(2 * nodes, K))
+    local2[:K, :] = tn(half(solved, 0), half(basis_in, 0))
+    each(1, N_CABLE, lambda d: snaps_trip(1, d, False).wait_recv())
+    local2[:K, :] += tn(half(snaps_in, 1), half(basis_out, 1))
     second.s0()
     second.s1()
     first.s4()
     first.s5()
     a[...] = total1[...] * scale_all
 
-    def send_snaps():
+    def spread_second():
         second.s3()
-        each(1, N_CABLE, lambda d: snaps_trip(d, True).start())
-        snaps_in[cable] = solved[cable]
-
-    factor_256(a, factor.at[:K, :K], inverse1, {16: second.s2, 28: send_snaps})
+        send_snaps(0)
+
+    factor_256(a, factor.at[:K, :K], inverse1, {12: second.s2, 24: spread_second})
     w1 = inverse1[...]
     w1_out[...] = w1.astype(BF16)
     factor[K:, :K] = jnp.zeros((K, K), F32)
@@ -460,7 +477,7 @@
     w2 = inverse2[...]
     w2_out[...] = w2.astype(BF16)
     cross_out[...] = (-nn(w2, t, HI)).astype(BF16)
-    each(1, N_CABLE, lambda d: snaps_trip(d, False).wait_recv())
+    each(1, N_CABLE, lambda d: snaps_trip(0, d, False).wait_recv())
 
     for h in range(2):
         rows32[h] = snaps_in[:, :, h * 128:(h + 1) * 128].astype(F32).reshape(positions * block, 128)
@@ -476,7 +493,8 @@
     second.drain()
     edges.wait_send()
     each(1, N_CABLE, lambda d: basis_trip(d, True).wait_send())
-    each(1, N_CABLE, lambda d: snaps_trip(d, True).wait_send())
+    for q in range(2):
+        each(1, N_CABLE, lambda d: snaps_trip(q, d, True).wait_send())
 
 
 def exchange_and_factor(rows_all, frames, tension, step_index, owner_map, basis, singular):
@@ -490,9 +508,11 @@
         lambda *refs: main_kernel(rows_all, *refs),
         out_shape=[jax.ShapeDtypeStruct((2 * K, 2 * K), F32), square, square, square,
                    jax.ShapeDtypeStruct((rows, SNAP), BF16)],
-        in_specs=[vmem_spec()] * 6,
+        in_specs=[pl.BlockSpec(memory_space=pltpu.HBM)] * 6,
         out_specs=[vmem_spec()] * 5,
         scratch_shapes=[
+            *[VMEM(x.shape, x.dtype) for x in (frames, tension, step_index, owner_map, basis, singular)],
+            dma((6,)),
             VMEM((4 * (nodes + 2 * EDGE), 128), F32),
             VMEM((2, 4 * EDGE, 128), BF16),
             VMEM((2, 2, 128), F32),
@@ -513,7 +533,7 @@
             VMEM((2 * K, K), F32),
             VMEM((2 * K, K), F32),
             *reduce_scratch(K), *reduce_scratch(2 * K),
-            dma((4,)), dma((4,)), *[dma((N_CABLE,))] * 4,
+            dma((4,)), dma((4,)), *[dma((2, N_CABLE))] * 4,
         ],
         compiler_params=pltpu.CompilerParams(collective_id=0, has_side_effects=True, vmem_limit_bytes=48 * 2**20),
         name="relax_exchange_factor",
@@ -549,8 +569,9 @@
     gain = singular[None, :]
     rows_all = basis.shape[0] * lax.axis_size("cable") * lax.axis_size("seg")
     lines = frames.reshape(nodes, 2, 2, 128).transpose(0, 2, 1, 3).reshape(4 * nodes, 128)
-    factor, w1, w2, cross, snaps = exchange_and_factor(
-        rows_all, lines, tension.T, step_index[None, :], owner_map[None, :], basis, gain)
+    operands = (pltpu.with_memory_space_constraint(value, pltpu.HBM) for value in (
+        lines, tension.T, step_index[None, :], owner_map[None, :], basis, gain))
+    factor, w1, w2, cross, snaps = exchange_and_factor(rows_all, *operands)
     factor, rotated = rotate(factor, w1, w2, cross, basis, gain, snaps)
     return factor, rotated.reshape(old_basis.shape[:3] + (2 * K,))
 

time: 90.9 us -> 74.9 us (0.82)
  the two profiles are of different devices: /device:TPU:3 before, /device:TPU:1 now
where the time goes in v4:
time: 74.9 us; the launch traced here: 74.8 us
  Pallas kernels  74 us (99%)
  between operations  0.83 us (1%)
    pallas_call x1, Pallas kernels, exchange_and_factor(): pl.pallas_call(lambda *refs: main_kernel(rows_all, *refs), out_shape=[jax...  71.6 us
    pallas_call x1, Pallas kernels, rotate(): pl.pallas_call(rotate_kernel, out_shape=[jax.ShapeDtypeStruct((width, wid...  2.4 us

profile of v4, /device:TPU:1, one launch (start us, length us, event | category | flops | bytes accessed | tf_op | source)
XLA Modules:
  0.0 74.8 jit_solution(9113100029325995890)
XLA Ops:
  0.6 0.0 copy-start.1
  0.6 0.0 copy-start
  0.7 71.6 %relax_exchange_factor.1 = (f32[512,512]{1,0:T(8,128)S(1)}, bf16[256,256]{1,0:T(8,128)(2,1)S(1)}, bf16[256,256]{1,0:T(8,128)(2,1)S(1)}, bf16[256,256]{1,0:T(8,128)(2,1)S(1)}, bf16[2048,256]{1,0:T(8,128)(2,1)S(1)}) custom-call(bf16[4096,128]{1,0:T(8,128)(2,1)} %bitcast.15, f32[2,1024]{1,0:T(2,128)} %bitcast.16, s32[1,256]{1,0:T(1,128)} %bitcast.17, ...), custom_call_target="tpu_custom_call" | custom-call | tf_op jit(solution)/shard_map/relax_exchange_factor/pallas_call | solution.py:507
  72.2 0.0 copy-done.1
  72.2 0.0 copy-done
  72.2 2.4 %rotate.1 = (f32[512,512]{1,0:T(8,128)}, bf16[2048,512]{1,0:T(8,128)(2,1)}) custom-call(f32[512,512]{1,0:T(8,128)S(1)} %get-tuple-element.9.factor_in, bf16[256,256]{1,0:T(8,128)(2,1)S(1)} %get-tuple-element.10.w1, bf16[256,256]{1,0:T(8,128)(2,1)S(1)} %get-tuple-element.11.w2, bf16[256,256]{1,0:T(8,128)(2,1)S(1)} %get-tuple-element.12.cross, ...), custom_call_target="tpu_custom_call" | custom-call | tf_op jit(solution)/shard_map/rotate/pallas_call | solution.py:555
Async XLA Ops:
  0.6 71.6 %copy-start.1 = (f32[256]{0:T(256)S(1)}, f32[256]{0:T(256)}, u32[]{:S(2)}) copy-start(f32[256]{0:T(256)} %param.11) | copy-start | bytes 3076
  0.6 71.6 %copy-start = (bf16[1,32,64,256]{3,2,1,0:T(8,128)(2,1)S(1)}, bf16[1,32,64,256]{3,2,1,0:T(8,128)(2,1)}, u32[]{:S(2)}) copy-start(bf16[1,32,64,256]{3,2,1,0:T(8,128)(2,1)} %param.10) | copy-start | bytes 3145732

commit v5 on v4

--- a/solution.py
+++ b/solution.py
@@ -459,15 +459,12 @@
     first.s5()
     a[...] = total1[...] * scale_all
 
-    def spread_second():
-        second.s3()
-        send_snaps(0)
-
-    factor_256(a, factor.at[:K, :K], inverse1, {12: second.s2, 24: spread_second})
+    factor_256(a, factor.at[:K, :K], inverse1, {12: second.s2, 24: second.s3})
     w1 = inverse1[...]
     w1_out[...] = w1.astype(BF16)
     factor[K:, :K] = jnp.zeros((K, K), F32)
     second.s4()
+    send_snaps(0)
     second.s5()
     low = nt(total2[:K, :] * scale_all, w1, HI)
     factor[:K, K:] = low.T

time: 74.9 us -> 70 us (0.935)
  Pallas kernels: 74 us -> 69.1 us
    pallas_call x1, Pallas kernels: 71.6 us -> 66.7 us  [exchange_and_factor(): pl.pallas_call(lambda *refs: main_kernel(rows_all, *refs), out_shape=[jax...]
where the time goes in v5:
time: 70 us; the launch traced here: 69.9 us
  Pallas kernels  69.1 us (99%)
  between operations  0.83 us (1%)
    pallas_call x1, Pallas kernels, exchange_and_factor(): pl.pallas_call(lambda *refs: main_kernel(rows_all, *refs), out_shape=[jax...  66.7 us
    pallas_call x1, Pallas kernels, rotate(): pl.pallas_call(rotate_kernel, out_shape=[jax.ShapeDtypeStruct((width, wid...  2.4 us

profile of v5, /device:TPU:1, one launch (start us, length us, event | category | flops | bytes accessed | tf_op | source)
XLA Modules:
  0.0 69.9 jit_solution(4496382580019614469)
XLA Ops:
  0.6 0.0 copy-start.1
  0.6 0.0 copy-start
  0.7 66.7 %relax_exchange_factor.1 = (f32[512,512]{1,0:T(8,128)S(1)}, bf16[256,256]{1,0:T(8,128)(2,1)S(1)}, bf16[256,256]{1,0:T(8,128)(2,1)S(1)}, bf16[256,256]{1,0:T(8,128)(2,1)S(1)}, bf16[2048,256]{1,0:T(8,128)(2,1)S(1)}) custom-call(bf16[4096,128]{1,0:T(8,128)(2,1)} %bitcast.15, f32[2,1024]{1,0:T(2,128)} %bitcast.16, s32[1,256]{1,0:T(1,128)} %bitcast.17, ...), custom_call_target="tpu_custom_call" | custom-call | tf_op jit(solution)/shard_map/relax_exchange_factor/pallas_call | solution.py:504
  67.3 0.0 copy-done.1
  67.4 0.0 copy-done
  67.4 2.4 %rotate.1 = (f32[512,512]{1,0:T(8,128)}, bf16[2048,512]{1,0:T(8,128)(2,1)}) custom-call(f32[512,512]{1,0:T(8,128)S(1)} %get-tuple-element.9.factor_in, bf16[256,256]{1,0:T(8,128)(2,1)S(1)} %get-tuple-element.10.w1, bf16[256,256]{1,0:T(8,128)(2,1)S(1)} %get-tuple-element.11.w2, bf16[256,256]{1,0:T(8,128)(2,1)S(1)} %get-tuple-element.12.cross, ...), custom_call_target="tpu_custom_call" | custom-call | tf_op jit(solution)/shard_map/rotate/pallas_call | solution.py:552
Async XLA Ops:
  0.6 66.7 %copy-start.1 = (f32[256]{0:T(256)S(1)}, f32[256]{0:T(256)}, u32[]{:S(2)}) copy-start(f32[256]{0:T(256)} %param.11) | copy-start | bytes 3076
  0.6 66.7 %copy-start = (bf16[1,32,64,256]{3,2,1,0:T(8,128)(2,1)S(1)}, bf16[1,32,64,256]{3,2,1,0:T(8,128)(2,1)}, u32[]{:S(2)}) copy-start(bf16[1,32,64,256]{3,2,1,0:T(8,128)(2,1)} %param.10) | copy-start | bytes 3145732

commit v6 on v5

--- a/solution.py
+++ b/solution.py
@@ -167,49 +167,69 @@
 
 def factor_128(a, upper, inverse, hooks=None, base=0):
     size, n = 8, 16
-    rows = lax.broadcasted_iota(jnp.int32, (size, 128), 0)
-    lanes = lax.broadcasted_iota(jnp.int32, (size, 128), 1)
+    tile = (size, 128)
+    rows = lax.broadcasted_iota(jnp.int32, tile, 0)
+    lanes = lax.broadcasted_iota(jnp.int32, tile, 1)
     depth = lax.broadcasted_iota(jnp.int32, (n, size, 128), 0)
     q = jnp.where(lanes[None] == rows[None] + size * depth, 1.0, 0.0).astype(F32)
+
+    def over_lanes(x, j):
+        return jnp.broadcast_to(x[..., j:j + 1], x.shape)
+
+    def over_rows(x):
+        return jnp.broadcast_to(x[:, None, :], (x.shape[0], size, 128))
+
     for kb in range(n):
         if hooks is not None and base + kb in hooks:
             hooks[base + kb]()
         at = size * kb
-        own, own_q = a[0], q[0]
-        a, q = a[1:], q[1:]
-        stack = lambda x: jnp.broadcast_to(x[:, None, :], (size, size, 128))
         rest = n - 1 - kb
-        r, s = stack(own), stack(own_q)
-        cols = [stack(jnp.broadcast_to(own[:, at + j:at + j + 1], (size, 128))) for j in range(size)]
-        side = [jnp.broadcast_to(a[:, :, at + k:at + k + 1], (rest, size, 128)) for k in range(size)] if rest else []
-        m, rr, ss, pivot, root = [], [], [], [], []
-        ut, wt = jnp.zeros((size, 128), F32), jnp.zeros((size, 128), F32)
+        own, own_q, a, q = a[0], q[0], a[1:], q[1:]
+        r, s = over_rows(own), over_rows(own_q)
+        cols = [over_rows(over_lanes(own, at + j)[j:]) for j in range(size)]
+        if rest:
+            near = [over_lanes(a[0], at + k) for k in range(size)]
+            next_a, next_q = a[0], q[0]
+        far = [over_lanes(a[1:], at + k) for k in range(size)] if rest > 1 else []
+        m, rr, ss, pivot = [], [], [], []
+        ut, wt = jnp.zeros(tile, F32), jnp.zeros(tile, F32)
         for k in range(size):
             d = cols[k][0]
             pivot.append(1.0 / d)
-            rr.append(r[0]); ss.append(s[0])
+            rr.append(r[0])
+            ss.append(s[0])
+            if rest:
+                scaled = near[k] * pivot[k]
+                next_a = next_a - scaled * r[0]
+                next_q = next_q - scaled * s[0]
+                for j in range(k + 1, size):
+                    near[j] = near[j] - scaled * cols[k][j - k]
             if k < size - 1:
                 below = cols[k][1:]
-                mk = below * pivot[k][None]
-                m.append(mk)
+                m.append(below * pivot[k][None])
                 for j in range(k + 1, size):
-                    cols[j] = cols[j][1:] if j == k + 1 and False else cols[j][1:] - mk * below[j - k - 1][None]
-                r = r[1:] - mk * r[0][None]
-                s = s[1:] - mk * s[0][None]
-            rt = lax.rsqrt(d)
-            ut = jnp.where(rows == k, rr[k] * rt, ut)
-            wt = jnp.where(rows == k, ss[k] * rt, wt)
-        z, zs = [None] * size, [None] * size
-        for k in reversed(range(size)):
-            zk, zsk = rr[k] * pivot[k], ss[k] * pivot[k]
-            for j in range(k + 1, size):
-                zk = zk - m[k][j - k - 1] * z[j]
-                zsk = zsk - m[k][j - k - 1] * zs[j]
-            z[k], zs[k] = zk, zsk
-        if rest:
+                    cols[j] = cols[j] - m[k][j - k - 1:] * below[j - k - 1][None]
+                r = r[1:] - m[k] * r[0][None]
+                s = s[1:] - m[k] * s[0][None]
+            root = lax.rsqrt(d)
+            ut = jnp.where(rows == k, rr[k] * root, ut)
+            wt = jnp.where(rows == k, ss[k] * root, wt)
+        if rest > 1:
+            z, zs = [None] * size, [None] * size
+            for k in reversed(range(size)):
+                zk, zsk = rr[k] * pivot[k], ss[k] * pivot[k]
+                for j in range(k + 1, size):
+                    zk = zk - m[k][j - k - 1] * z[j]
+                    zsk = zsk - m[k][j - k - 1] * zs[j]
+                z[k], zs[k] = zk, zsk
+            far_a, far_q = a[1:], q[1:]
             for k in range(size):
-                a = a - side[k] * z[k][None]
-                q = q - side[k] * zs[k][None]
+                far_a = far_a - far[k] * z[k][None]
+                far_q = far_q - far[k] * zs[k][None]
+            a = jnp.concatenate([next_a[None], far_a])
+            q = jnp.concatenate([next_q[None], far_q])
+        elif rest:
+            a, q = next_a[None], next_q[None]
         upper[at:at + size, :] = jnp.where(lanes >= rows + at, ut, 0.0)
         inverse[at:at + size, :] = jnp.where(lanes <= rows + at, wt, 0.0)
 
@@ -357,15 +377,15 @@
     def pack(b, _):
         rows = pl.ds(pl.multiple_of(b * block, block), block)
         for h in range(2):
-            solved[b, q * block:(q + 1) * block, h * 128:(h + 1) * 128] = solved32[h, rows, :].astype(BF16)
+            solved[q, b, :, h * 128:(h + 1) * 128] = solved32[h, rows, :].astype(BF16)
         return 0
 
     lax.fori_loop(0, N_CABLE, pack, 0)
 
 
 def main_kernel(rows_all, frames_in, tension_in, step_in, owner_in, basis_hbm, singular_in,
-                factor, w1_out, w2_out, cross_out, snaps,
-                frames, tension, step_index, owner, basis, singular, load_sem, padded, halo, tens_halo, tens_rows, weights, solved32, solved, scaled, rows32, basis_out, basis_in,
+                factor, w1_out, w2_out, cross_out, snaps, scaled,
+                frames, tension, step_index, owner, basis, singular, load_sem, padded, halo, tens_halo, tens_rows, weights, solved32, solved, rows32, basis_out, basis_in,
                 snaps_in, a, inverse1, inverse2, local1, total1, local2, total2, half1, parts1, lines1, send1, recv1,
                 half2, parts2, lines2, send2, recv2, halo_send, halo_recv, b_send, b_recv, s_send, s_recv):
     cable, seg = lax.axis_index("cable"), lax.axis_index("seg")
@@ -384,20 +404,24 @@
     for load in loads[:3]:
         load.wait()
     scaled[...] = (basis[...].astype(F32) * singular[...]).astype(BF16)
-    pick = (lax.broadcasted_iota(jnp.int32, (positions, positions), 0) == owner[...]).astype(F32)
+    line = lax.broadcasted_iota(jnp.int32, (positions, positions), 0)
+    pick = (2 * lax.rem(line, N_CABLE) + line // N_CABLE == owner[...]).astype(F32)
     pick_bf = pick.astype(BF16)
-    unpick_bf = pick.T.astype(BF16)
-
-    def by_streamer(n, _):
-        rows = scaled[pl.ds(pl.multiple_of(n * positions, positions), positions), :]
-        moved = nn(pick_bf, rows)
+
+    def by_streamer(q):
+        def turn(n, _):
+            rows = scaled[pl.ds(pl.multiple_of(n * positions, positions), positions), :]
+            moved = nn(pick_bf[q * N_CABLE:(q + 1) * N_CABLE], rows)
+            for h in range(2):
+                rows32[h, pl.ds(q * nodes + n, N_CABLE, stride=block), :] = moved[:, h * 128:(h + 1) * 128]
+            return 0
+
+        lax.fori_loop(0, block, turn, 0, unroll=8)
         for h in range(2):
-            rows32[h, pl.ds(n, positions, stride=block), :] = moved[:, h * 128:(h + 1) * 128]
-        return 0
-
-    lax.fori_loop(0, block, by_streamer, 0, unroll=4)
-    for h in range(2):
-        basis_out[:, :, h * 128:(h + 1) * 128] = rows32[h].astype(BF16).reshape(N_CABLE, 2 * block, 128)
+            basis_out[q, :, :, h * 128:(h + 1) * 128] = (
+                rows32[h, q * nodes:(q + 1) * nodes, :].astype(BF16).reshape(N_CABLE, block, 128))
+
+    by_streamer(0)
     for load in loads[3:]:
         load.wait()
     first = Reduce(local1, total1, half1, parts1, lines1, (send1, recv1))
@@ -407,9 +431,8 @@
 
     def exchange(d, out, into, q, send, recv, mine):
         peer = lax.rem(cable + d, N_CABLE)
-        rows = pl.ds(q * block, block)
         return pltpu.make_async_remote_copy(
-            src_ref=out.at[peer, rows, :], dst_ref=into.at[cable if mine else peer, rows, :], send_sem=send.at[q, d],
+            src_ref=out.at[q, peer], dst_ref=into.at[q, cable if mine else peer], send_sem=send.at[q, d],
             recv_sem=recv.at[q, cable if mine else peer], device_id=(peer, seg), device_id_type=MESH)
 
     def basis_trip(d, mine):
@@ -420,22 +443,23 @@
 
     def send_snaps(q):
         each(1, N_CABLE, lambda d: snaps_trip(q, d, True).start())
-        snaps_in[cable, q * block:(q + 1) * block, :] = solved[cable, q * block:(q + 1) * block, :]
+        snaps_in[q, cable] = solved[q, cable]
 
     def half(ref, q):
-        return ref[:, q * block:(q + 1) * block, :].reshape(nodes, K)
+        return ref[q].reshape(nodes, K)
 
     met()
     edges.start()
     each(1, N_CABLE, lambda d: basis_trip(d, True).start())
     local1[...] = tn(scaled[...], scaled[...])
     first.s0()
-    basis_in[cable, 0:block, :] = basis_out[cable, 0:block, :]
+    basis_in[0, cable] = basis_out[0, cable]
     padded[4 * EDGE:4 * (EDGE + nodes), :] = frames[...].astype(F32)
     for q in range(2):
         for s in range(STRIPS):
             tens_rows[q, 8 + s:9 + s, :] = tension[q:q + 1, s * strip:(s + 1) * strip]
     first.s1()
+    by_streamer(1)
     edges.wait_recv()
     padded[0:4 * EDGE, :] = halo[0].astype(F32)
     padded[4 * (EDGE + nodes):, :] = halo[1].astype(F32)
@@ -443,8 +467,8 @@
     stiff = DRAG_RATE * (1.0 + step_index[...].astype(F32))
     scale = [jnp.broadcast_to(stiff[:, h * 128:(h + 1) * 128], (STRIPS, 128)) for h in range(2)]
     relax(1, scale, padded, weights, solved32, solved, strip, block)
+    first.s2()
     send_snaps(1)
-    first.s2()
     relax(0, scale, padded, weights, solved32, solved, strip, block)
     flat = solved[...].reshape(2 * nodes, SNAP)
     local2[K:, :] = tn(flat, flat)
@@ -477,7 +501,9 @@
     each(1, N_CABLE, lambda d: snaps_trip(0, d, False).wait_recv())
 
     for h in range(2):
-        rows32[h] = snaps_in[:, :, h * 128:(h + 1) * 128].astype(F32).reshape(positions * block, 128)
+        rows32[h] = snaps_in[:, :, :, h * 128:(h + 1) * 128].astype(F32).reshape(positions * block, 128)
+
+    unpick_bf = pick.T.astype(BF16)
 
     def by_position(n, _):
         rows = jnp.concatenate([rows32[h, pl.ds(n, positions, stride=block), :] for h in range(2)], axis=1)
@@ -485,7 +511,7 @@
             nn(unpick_bf, rows.astype(BF16)).astype(BF16))
         return 0
 
-    lax.fori_loop(0, block, by_position, 0, unroll=4)
+    lax.fori_loop(0, block, by_position, 0, unroll=8)
     first.drain()
     second.drain()
     edges.wait_send()
@@ -504,9 +530,9 @@
     return pl.pallas_call(
         lambda *refs: main_kernel(rows_all, *refs),
         out_shape=[jax.ShapeDtypeStruct((2 * K, 2 * K), F32), square, square, square,
-                   jax.ShapeDtypeStruct((rows, SNAP), BF16)],
+                   jax.ShapeDtypeStruct((rows, SNAP), BF16), jax.ShapeDtypeStruct((rows, K), BF16)],
         in_specs=[pl.BlockSpec(memory_space=pltpu.HBM)] * 6,
-        out_specs=[vmem_spec()] * 5,
+        out_specs=[vmem_spec()] * 6,
         scratch_shapes=[
             *[VMEM(x.shape, x.dtype) for x in (frames, tension, step_index, owner_map, basis, singular)],
             dma((6,)),
@@ -516,12 +542,11 @@
             VMEM((2, 24, 128), F32),
             VMEM((2, 2, steps, STRIPS, 128), F32),
             VMEM((2, nodes, 128), F32),
-            VMEM((N_CABLE, 2 * block, SNAP), BF16),
-            VMEM((rows, K), BF16),
+            VMEM((2, N_CABLE, block, SNAP), BF16),
             VMEM((2, rows, 128), F32),
-            VMEM((N_CABLE, 2 * block, K), BF16),
-            VMEM((N_CABLE, 2 * block, K), BF16),
-            VMEM((N_CABLE, 2 * block, SNAP), BF16),
+            VMEM((2, N_CABLE, block, K), BF16),
+            VMEM((2, N_CABLE, block, K), BF16),
+            VMEM((2, N_CABLE, block, SNAP), BF16),
             VMEM((K, K), F32),
             VMEM((K, K), F32),
             VMEM((K, K), F32),
@@ -537,27 +562,25 @@
     )(frames, tension, step_index, owner_map, basis, singular)
 
 
-def rotate_kernel(factor_in, w1, w2, cross, basis, singular, snaps, factor, new_basis, sem):
+def rotate_kernel(factor_in, w1, w2, cross, scaled, snaps, factor, new_basis, sem):
     copy = pltpu.make_async_copy(factor_in, factor, sem)
     copy.start()
-    scaled = (basis[...].astype(F32) * singular[...]).astype(BF16)
-    new_basis[:, :K] = nt(scaled, w1[...]).astype(BF16)
-    new_basis[:, K:] = (nt(scaled, cross[...]) + nt(snaps[...], w2[...])).astype(BF16)
+    new_basis[:, :K] = nt(scaled[...], w1[...]).astype(BF16)
+    new_basis[:, K:] = (nt(scaled[...], cross[...]) + nt(snaps[...], w2[...])).astype(BF16)
     copy.wait()
 
 
-def rotate(factor, w1, w2, cross, basis, singular, snaps):
-    rows, width = basis.shape[0], 2 * K
-    anywhere = pl.BlockSpec(memory_space=pl.ANY)
+def rotate(factor, w1, w2, cross, scaled, snaps):
+    rows, width = scaled.shape[0], 2 * K
     return pl.pallas_call(
         rotate_kernel,
         out_shape=[jax.ShapeDtypeStruct((width, width), F32), jax.ShapeDtypeStruct((rows, width), BF16)],
-        in_specs=[anywhere] + [vmem_spec()] * 6,
-        out_specs=[anywhere, vmem_spec()],
+        in_specs=[vmem_spec()] * 6,
+        out_specs=[pl.BlockSpec(memory_space=pltpu.HBM), vmem_spec()],
         scratch_shapes=[pltpu.SemaphoreType.DMA],
         compiler_params=pltpu.CompilerParams(vmem_limit_bytes=40 * 2**20),
         name="rotate",
-    )(factor, w1, w2, cross, basis, singular, snaps)
+    )(factor, w1, w2, cross, scaled, snaps)
 
 
 def body(frames, tension, step_index, owner_map, old_basis, singular):
@@ -568,8 +591,8 @@
     lines = frames.reshape(nodes, 2, 2, 128).transpose(0, 2, 1, 3).reshape(4 * nodes, 128)
     operands = (pltpu.with_memory_space_constraint(value, pltpu.HBM) for value in (
         lines, tension.T, step_index[None, :], owner_map[None, :], basis, gain))
-    factor, w1, w2, cross, snaps = exchange_and_factor(rows_all, *operands)
-    factor, rotated = rotate(factor, w1, w2, cross, basis, gain, snaps)
+    factor, w1, w2, cross, snaps, scaled = exchange_and_factor(rows_all, *operands)
+    factor, rotated = rotate(factor, w1, w2, cross, scaled, snaps)
     return factor, rotated.reshape(old_basis.shape[:3] + (2 * K,))
 
 

time: 70 us -> 67.6 us (0.966)
  Pallas kernels: 69.1 us -> 66.7 us
    pallas_call x1, Pallas kernels: 66.7 us -> 64.2 us  [exchange_and_factor(): pl.pallas_call(lambda *refs: main_kernel(rows_all, *refs), out_shape=[jax...]
where the time goes in v6:
time: 67.6 us; the launch traced here: 67.5 us
  Pallas kernels  66.7 us (99%)
  between operations  0.8 us (1%)
    pallas_call x1, Pallas kernels, exchange_and_factor(): pl.pallas_call(lambda *refs: main_kernel(rows_all, *refs), out_shape=[jax...  64.2 us
    pallas_call x1, Pallas kernels, rotate(): pl.pallas_call(rotate_kernel, out_shape=[jax.ShapeDtypeStruct((width, wid...  2.53 us

profile of v6, /device:TPU:1, one launch (start us, length us, event | category | flops | bytes accessed | tf_op | source)
XLA Modules:
  0.0 67.5 jit_solution(14742242085170037307)
XLA Ops:
  0.6 64.2 %relax_exchange_factor.1 = (f32[512,512]{1,0:T(8,128)S(1)}, bf16[256,256]{1,0:T(8,128)(2,1)S(1)}, bf16[256,256]{1,0:T(8,128)(2,1)S(1)}, bf16[256,256]{1,0:T(8,12...) custom-call(bf16[4096,128]{1,0:T(8,128)(2,1)} %bitcast.11, f32[2,1024]{1,0:T(2,128)} %bitcast.13, ...), custom_call_target="tpu_custom_call" | custom-call | tf_op jit(solution)/shard_map/relax_exchange_factor/pallas_call | solution.py:530
  64.8 2.5 %rotate.1 = (f32[512,512]{1,0:T(8,128)}, bf16[2048,512]{1,0:T(8,128)(2,1)}) custom-call(f32[512,512]{1,0:T(8,128)S(1)} %get-tuple-element.10.factor_in, bf16[256,256]{1,0:T(8,128)(2,1)S(1)} %get-tuple-element.11.w1, bf16[256,256]{1,0:T(8,128)(2,1)S(1)} %get-tuple-element.12.w2, bf16[256,256]{1,0:T(8,128)(2,1)S(1)} %get-tuple-element.13.cross, ...), custom_call_target="tpu_custom_call" | custom-call | tf_op jit(solution)/shard_map/rotate/pallas_call | solution.py:575

commit v7 on v6

--- a/solution.py
+++ b/solution.py
@@ -101,21 +101,30 @@
     def c1(self):
         return self.copy(self.local.at[self.other_half(), :], self.half, 0, 0, self.sister)
 
-    def p1(self, d, mine):
+    def p1(self, d):
         spot, device = self.plane(d)
         return self.copy(self.half.at[pl.ds(pl.multiple_of(spot * self.depth, self.depth), self.depth), :],
-                         self.parts.at[self.spot if mine else spot], 16 + d, 16 + (self.spot if mine else spot), device)
-
-    def l1(self, d, mine):
+                         self.parts.at[self.spot], 2, 2, device)
+
+    def p1_all(self):
+        return self.copy(self.half.at[pl.ds(0, (PLANE - 1) * self.depth), :], self.parts.at[pl.ds(0, PLANE - 1)],
+                         2, 2, self.sister)
+
+    def l1(self, d):
         y, device = self.line(d)
-        return self.copy(self.lines.at[self.y], self.lines.at[self.y if mine else y], 4 + d,
-                         4 + (self.y if mine else y), device)
-
-    def p2(self, d, mine):
+        return self.copy(self.lines.at[self.y], self.lines.at[self.y], 4, 4, device)
+
+    def l1_all(self):
+        return self.copy(self.lines.at[pl.ds(0, 3)], self.lines.at[pl.ds(0, 3)], 4, 4, self.sister)
+
+    def p2(self, d):
         spot, device = self.plane(d)
-        rows = self.part(self.spot if mine else spot)
-        return self.copy(self.total.at[rows, :], self.total.at[rows, :], 32 + d,
-                         32 + (self.spot if mine else spot), device)
+        rows = self.part(self.spot)
+        return self.copy(self.total.at[rows, :], self.total.at[rows, :], 3, 3, device)
+
+    def p2_all(self):
+        rows = pl.ds(0, (PLANE - 1) * self.depth)
+        return self.copy(self.total.at[rows, :], self.total.at[rows, :], 3, 3, self.sister)
 
     def c2(self, mine):
         rows = self.own_half() if mine else self.other_half()
@@ -127,42 +136,39 @@
     def s1(self):
         self.c1().wait_recv()
         self.half[...] = self.half[...] + self.local[self.own_half(), :]
-        each(1, PLANE, lambda d: self.p1(d, True).start())
+        each(1, PLANE, lambda d: self.p1(d).start())
         self.parts[self.spot] = self.half[pl.ds(pl.multiple_of(self.spot * self.depth, self.depth), self.depth), :]
 
     def s2(self):
-        each(1, PLANE, lambda d: self.p1(d, False).wait_recv())
+        self.p1_all().wait_recv()
         acc = self.parts[0]
         for i in range(1, PLANE):
             acc = acc + self.parts[i]
         self.lines[self.y] = acc
-        each(1, 4, lambda d: self.l1(d, True).start())
+        each(1, 4, lambda d: self.l1(d).start())
 
     def s3(self):
-        each(1, 4, lambda d: self.l1(d, False).wait_recv())
+        self.l1_all().wait_recv()
         acc = (self.lines[0] + self.lines[1]) + (self.lines[2] + self.lines[3])
         self.total[self.part(self.spot), :] = acc
-        each(1, PLANE, lambda d: self.p2(d, True).start())
+        each(1, PLANE, lambda d: self.p2(d).start())
 
     def s4(self):
-        each(1, PLANE, lambda d: self.p2(d, False).wait_recv())
+        self.p2_all().wait_recv()
         self.c2(True).start()
 
     def s5(self):
         self.c2(False).wait_recv()
 
     def drain(self):
-        self.c1().wait_send()
-        each(1, PLANE, lambda d: self.p1(d, True).wait_send())
-        each(1, 4, lambda d: self.l1(d, True).wait_send())
-        each(1, PLANE, lambda d: self.p2(d, True).wait_send())
-        self.c2(True).wait_send()
+        for copy in (self.c1(), self.p1_all(), self.l1_all(), self.p2_all(), self.c2(True)):
+            copy.wait_send()
 
 
 def reduce_scratch(rows):
     depth = rows // 2 // PLANE
     return [VMEM((rows // 2, K), F32), VMEM((PLANE, depth, K), F32), VMEM((4, depth, K), F32),
-            pltpu.SemaphoreType.DMA((48,)), pltpu.SemaphoreType.DMA((48,))]
+            pltpu.SemaphoreType.DMA((5,)), pltpu.SemaphoreType.DMA((5,))]
 
 
 def factor_128(a, upper, inverse, hooks=None, base=0):
@@ -429,20 +435,26 @@
     edges = Halo(frames, tension, halo, tens_halo, halo_send, halo_recv)
     edges.zero_ends()
 
-    def exchange(d, out, into, q, send, recv, mine):
+    def exchange(d, out, into, q, send, recv):
         peer = lax.rem(cable + d, N_CABLE)
         return pltpu.make_async_remote_copy(
-            src_ref=out.at[q, peer], dst_ref=into.at[q, cable if mine else peer], send_sem=send.at[q, d],
-            recv_sem=recv.at[q, cable if mine else peer], device_id=(peer, seg), device_id_type=MESH)
-
-    def basis_trip(d, mine):
-        return exchange(d, basis_out, basis_in, 0, b_send, b_recv, mine)
-
-    def snaps_trip(q, d, mine):
-        return exchange(d, solved, snaps_in, q, s_send, s_recv, mine)
+            src_ref=out.at[q, peer], dst_ref=into.at[q, cable], send_sem=send.at[q], recv_sem=recv.at[q],
+            device_id=(peer, seg), device_id_type=MESH)
+
+    def exchange_all(out, into, q, send, recv):
+        pieces = pl.ds(0, N_CABLE - 1)
+        return pltpu.make_async_remote_copy(
+            src_ref=out.at[q, pieces], dst_ref=into.at[q, pieces], send_sem=send.at[q], recv_sem=recv.at[q],
+            device_id=(lax.rem(cable + 1, N_CABLE), seg), device_id_type=MESH)
+
+    def basis_all():
+        return exchange_all(basis_out, basis_in, 0, b_send, b_recv)
+
+    def snaps_all(q):
+        return exchange_all(solved, snaps_in, q, s_send, s_recv)
 
     def send_snaps(q):
-        each(1, N_CABLE, lambda d: snaps_trip(q, d, True).start())
+        each(1, N_CABLE, lambda d: exchange(d, solved, snaps_in, q, s_send, s_recv).start())
         snaps_in[q, cable] = solved[q, cable]
 
     def half(ref, q):
@@ -450,7 +462,7 @@
 
     met()
     edges.start()
-    each(1, N_CABLE, lambda d: basis_trip(d, True).start())
+    each(1, N_CABLE, lambda d: exchange(d, basis_out, basis_in, 0, b_send, b_recv).start())
     local1[...] = tn(scaled[...], scaled[...])
     first.s0()
     basis_in[0, cable] = basis_out[0, cable]
@@ -473,9 +485,9 @@
     flat = solved[...].reshape(2 * nodes, SNAP)
     local2[K:, :] = tn(flat, flat)
     first.s3()
-    each(1, N_CABLE, lambda d: basis_trip(d, False).wait_recv())
+    basis_all().wait_recv()
     local2[:K, :] = tn(half(solved, 0), half(basis_in, 0))
-    each(1, N_CABLE, lambda d: snaps_trip(1, d, False).wait_recv())
+    snaps_all(1).wait_recv()
     local2[:K, :] += tn(half(snaps_in, 1), half(basis_out, 1))
     second.s0()
     second.s1()
@@ -483,7 +495,7 @@
     first.s5()
     a[...] = total1[...] * scale_all
 
-    factor_256(a, factor.at[:K, :K], inverse1, {12: second.s2, 24: second.s3})
+    factor_256(a, factor.at[:K, :K], inverse1, {14: second.s2, 23: second.s3})
     w1 = inverse1[...]
     w1_out[...] = w1.astype(BF16)
     factor[K:, :K] = jnp.zeros((K, K), F32)
@@ -498,7 +510,7 @@
     w2 = inverse2[...]
     w2_out[...] = w2.astype(BF16)
     cross_out[...] = (-nn(w2, t, HI)).astype(BF16)
-    each(1, N_CABLE, lambda d: snaps_trip(0, d, False).wait_recv())
+    snaps_all(0).wait_recv()
 
     for h in range(2):
         rows32[h] = snaps_in[:, :, :, h * 128:(h + 1) * 128].astype(F32).reshape(positions * block, 128)
@@ -515,9 +527,9 @@
     first.drain()
     second.drain()
     edges.wait_send()
-    each(1, N_CABLE, lambda d: basis_trip(d, True).wait_send())
+    basis_all().wait_send()
     for q in range(2):
-        each(1, N_CABLE, lambda d: snaps_trip(q, d, True).wait_send())
+        snaps_all(q).wait_send()
 
 
 def exchange_and_factor(rows_all, frames, tension, step_index, owner_map, basis, singular):
@@ -555,7 +567,7 @@
             VMEM((2 * K, K), F32),
             VMEM((2 * K, K), F32),
             *reduce_scratch(K), *reduce_scratch(2 * K),
-            dma((4,)), dma((4,)), *[dma((2, N_CABLE))] * 4,
+            dma((4,)), dma((4,)), *[dma((2,))] * 4,
         ],
         compiler_params=pltpu.CompilerParams(collective_id=0, has_side_effects=True, vmem_limit_bytes=48 * 2**20),
         name="relax_exchange_factor",

time: 67.6 us -> 62.2 us (0.920)
  Pallas kernels: 66.7 us -> 61.3 us
    pallas_call x1, Pallas kernels: 64.2 us -> 58.8 us  [exchange_and_factor(): pl.pallas_call(lambda *refs: main_kernel(rows_all, *refs), out_shape=[jax...]
where the time goes in v7:
time: 62.2 us; the launch traced here: 62.1 us
  Pallas kernels  61.3 us (99%)
  between operations  0.8 us (1%)
    pallas_call x1, Pallas kernels, exchange_and_factor(): pl.pallas_call(lambda *refs: main_kernel(rows_all, *refs), out_shape=[jax...  58.8 us
    pallas_call x1, Pallas kernels, rotate(): pl.pallas_call(rotate_kernel, out_shape=[jax.ShapeDtypeStruct((width, wid...  2.52 us

profile of v7, /device:TPU:1, one launch (start us, length us, event | category | flops | bytes accessed | tf_op | source)
XLA Modules:
  0.0 62.1 jit_solution(14004977947616055289)
XLA Ops:
  0.6 58.8 %relax_exchange_factor.1 = (f32[512,512]{1,0:T(8,128)S(1)}, bf16[256,256]{1,0:T(8,128)(2,1)S(1)}, bf16[256,256]{1,0:T(8,128)(2,1)S(1)}, bf16[256,256]{1,0:T(8,12...) custom-call(bf16[4096,128]{1,0:T(8,128)(2,1)} %bitcast.11, f32[2,1024]{1,0:T(2,128)} %bitcast.13, ...), custom_call_target="tpu_custom_call" | custom-call | tf_op jit(solution)/shard_map/relax_exchange_factor/pallas_call | solution.py:542
  59.4 2.5 %rotate.1 = (f32[512,512]{1,0:T(8,128)}, bf16[2048,512]{1,0:T(8,128)(2,1)}) custom-call(f32[512,512]{1,0:T(8,128)S(1)} %get-tuple-element.10.factor_in, bf16[256,256]{1,0:T(8,128)(2,1)S(1)} %get-tuple-element.11.w1, bf16[256,256]{1,0:T(8,128)(2,1)S(1)} %get-tuple-element.12.w2, bf16[256,256]{1,0:T(8,128)(2,1)S(1)} %get-tuple-element.13.cross, ...), custom_call_target="tpu_custom_call" | custom-call | tf_op jit(solution)/shard_map/rotate/pallas_call | solution.py:587

commit v8 on v7

--- a/solution.py
+++ b/solution.py
@@ -391,9 +391,9 @@
 
 def main_kernel(rows_all, frames_in, tension_in, step_in, owner_in, basis_hbm, singular_in,
                 factor, w1_out, w2_out, cross_out, snaps, scaled,
-                frames, tension, step_index, owner, basis, singular, load_sem, padded, halo, tens_halo, tens_rows, weights, solved32, solved, rows32, basis_out, basis_in,
-                snaps_in, a, inverse1, inverse2, local1, total1, local2, total2, half1, parts1, lines1, send1, recv1,
-                half2, parts2, lines2, send2, recv2, halo_send, halo_recv, b_send, b_recv, s_send, s_recv):
+                frames, tension, step_index, owner, basis, singular, load_sem, padded, halo, tens_halo, tens_rows, weights, solved32, solved, odd_rows, rows32, basis_out, basis_in,
+                snaps_in, a, inverse1, inverse2, local1, total1, local2, total2, local3, total3, half1, parts1, lines1, send1, recv1,
+                half2, parts2, lines2, send2, recv2, half3, parts3, lines3, send3, recv3, halo_send, halo_recv, b_send, b_recv, s_send, s_recv):
     cable, seg = lax.axis_index("cable"), lax.axis_index("seg")
     nodes = frames_in.shape[0] // 4
     strip = nodes // STRIPS
@@ -431,7 +431,8 @@
     for load in loads[3:]:
         load.wait()
     first = Reduce(local1, total1, half1, parts1, lines1, (send1, recv1))
-    second = Reduce(local2, total2, half2, parts2, lines2, (send2, recv2))
+    own = Reduce(local2, total2, half2, parts2, lines2, (send2, recv2))
+    mixed = Reduce(local3, total3, half3, parts3, lines3, (send3, recv3))
     edges = Halo(frames, tension, halo, tens_halo, halo_send, halo_recv)
     edges.zero_ends()
 
@@ -471,7 +472,6 @@
         for s in range(STRIPS):
             tens_rows[q, 8 + s:9 + s, :] = tension[q:q + 1, s * strip:(s + 1) * strip]
     first.s1()
-    by_streamer(1)
     edges.wait_recv()
     padded[0:4 * EDGE, :] = halo[0].astype(F32)
     padded[4 * (EDGE + nodes):, :] = halo[1].astype(F32)
@@ -481,30 +481,52 @@
     relax(1, scale, padded, weights, solved32, solved, strip, block)
     first.s2()
     send_snaps(1)
+    by_streamer(1)
     relax(0, scale, padded, weights, solved32, solved, strip, block)
     flat = solved[...].reshape(2 * nodes, SNAP)
-    local2[K:, :] = tn(flat, flat)
+    local2[...] = tn(flat, flat)
+    own.s0()
     first.s3()
+    own.s1()
     basis_all().wait_recv()
-    local2[:K, :] = tn(half(solved, 0), half(basis_in, 0))
+    local3[...] = tn(half(solved, 0), half(basis_in, 0))
     snaps_all(1).wait_recv()
-    local2[:K, :] += tn(half(snaps_in, 1), half(basis_out, 1))
-    second.s0()
-    second.s1()
+    local3[...] += tn(half(snaps_in, 1), half(basis_out, 1))
+    mixed.s0()
+    mixed.s1()
     first.s4()
     first.s5()
     a[...] = total1[...] * scale_all
 
-    factor_256(a, factor.at[:K, :K], inverse1, {14: second.s2, 23: second.s3})
+    factor_256(a, factor.at[:K, :K], inverse1, {4: own.s2, 16: mixed.s2, 17: own.s3, 26: mixed.s3})
     w1 = inverse1[...]
     w1_out[...] = w1.astype(BF16)
     factor[K:, :K] = jnp.zeros((K, K), F32)
-    second.s4()
+    unpick_bf = pick.T.astype(BF16)
+
+    def put_in_order(q):
+        for h in range(2):
+            rows32[h, q * nodes:(q + 1) * nodes, :] = (
+                snaps_in[q, :, :, h * 128:(h + 1) * 128].astype(F32).reshape(nodes, 128))
+
+    put_in_order(1)
+
+    def odd_by_position(n, _):
+        for h in range(2):
+            rows = rows32[h, pl.ds(nodes + n, N_CABLE, stride=block), :].astype(BF16)
+            odd_rows[pl.ds(pl.multiple_of(n * positions, positions), positions), h * 128:(h + 1) * 128] = (
+                nn(unpick_bf[:, N_CABLE:], rows))
+        return 0
+
+    lax.fori_loop(0, block, odd_by_position, 0, unroll=8)
+    own.s4()
+    mixed.s4()
     send_snaps(0)
-    second.s5()
-    low = nt(total2[:K, :] * scale_all, w1, HI)
+    own.s5()
+    mixed.s5()
+    low = nt(total3[...] * scale_all, w1, HI)
     factor[:K, K:] = low.T
-    a[...] = total2[K:, :] * scale_all - nt(low, low, HI)
+    a[...] = total2[...] * scale_all - nt(low, low, HI)
     t = nn(low, w1, HI)
     factor_256(a, factor.at[K:, K:], inverse2)
     w2 = inverse2[...]
@@ -512,20 +534,20 @@
     cross_out[...] = (-nn(w2, t, HI)).astype(BF16)
     snaps_all(0).wait_recv()
 
-    for h in range(2):
-        rows32[h] = snaps_in[:, :, :, h * 128:(h + 1) * 128].astype(F32).reshape(positions * block, 128)
-
-    unpick_bf = pick.T.astype(BF16)
+    put_in_order(0)
 
     def by_position(n, _):
-        rows = jnp.concatenate([rows32[h, pl.ds(n, positions, stride=block), :] for h in range(2)], axis=1)
-        snaps[pl.ds(pl.multiple_of(n * positions, positions), positions), :] = (
-            nn(unpick_bf, rows.astype(BF16)).astype(BF16))
+        for h in range(2):
+            rows = rows32[h, pl.ds(n, N_CABLE, stride=block), :].astype(BF16)
+            spot = pl.ds(pl.multiple_of(n * positions, positions), positions)
+            cols = slice(h * 128, (h + 1) * 128)
+            snaps[spot, cols] = (nn(unpick_bf[:, :N_CABLE], rows) + odd_rows[spot, cols]).astype(BF16)
         return 0
 
     lax.fori_loop(0, block, by_position, 0, unroll=8)
     first.drain()
-    second.drain()
+    own.drain()
+    mixed.drain()
     edges.wait_send()
     basis_all().wait_send()
     for q in range(2):
@@ -555,6 +577,7 @@
             VMEM((2, 2, steps, STRIPS, 128), F32),
             VMEM((2, nodes, 128), F32),
             VMEM((2, N_CABLE, block, SNAP), BF16),
+            VMEM((rows, SNAP), F32),
             VMEM((2, rows, 128), F32),
             VMEM((2, N_CABLE, block, K), BF16),
             VMEM((2, N_CABLE, block, K), BF16),
@@ -564,9 +587,8 @@
             VMEM((K, K), F32),
             VMEM((K, K), F32),
             VMEM((K, K), F32),
-            VMEM((2 * K, K), F32),
-            VMEM((2 * K, K), F32),
-            *reduce_scratch(K), *reduce_scratch(2 * K),
+            *[VMEM((K, K), F32)] * 4,
+            *reduce_scratch(K), *reduce_scratch(K), *reduce_scratch(K),
             dma((4,)), dma((4,)), *[dma((2,))] * 4,
         ],
         compiler_params=pltpu.CompilerParams(collective_id=0, has_side_effects=True, vmem_limit_bytes=48 * 2**20),

time: 62.2 us -> 60.2 us (0.968)
  Pallas kernels: 61.3 us -> 59.2 us
    pallas_call x1, Pallas kernels: 58.8 us -> 56.7 us  [exchange_and_factor(): pl.pallas_call(lambda *refs: main_kernel(rows_all, *refs), out_shape=[jax...]
where the time goes in v8:
time: 60.2 us; the launch traced here: 60 us
  Pallas kernels  59.2 us (98%)
  between operations  0.8 us (1%)
    pallas_call x1, Pallas kernels, exchange_and_factor(): pl.pallas_call(lambda *refs: main_kernel(rows_all, *refs), out_shape=[jax...  56.7 us
    pallas_call x1, Pallas kernels, rotate(): pl.pallas_call(rotate_kernel, out_shape=[jax.ShapeDtypeStruct((width, wid...  2.52 us

profile of v8, /device:TPU:1, one launch (start us, length us, event | category | flops | bytes accessed | tf_op | source)
XLA Modules:
  0.0 60.0 jit_solution(17305362370502726934)
XLA Ops:
  0.6 56.7 %relax_exchange_factor.1 = (f32[512,512]{1,0:T(8,128)S(1)}, bf16[256,256]{1,0:T(8,128)(2,1)S(1)}, bf16[256,256]{1,0:T(8,128)(2,1)S(1)}, bf16[256,256]{1,0:T(8,12...) custom-call(bf16[4096,128]{1,0:T(8,128)(2,1)} %bitcast.11, f32[2,1024]{1,0:T(2,128)} %bitcast.13, ...), custom_call_target="tpu_custom_call" | custom-call | tf_op jit(solution)/shard_map/relax_exchange_factor/pallas_call | solution.py:564
  57.3 2.5 %rotate.1 = (f32[512,512]{1,0:T(8,128)}, bf16[2048,512]{1,0:T(8,128)(2,1)}) custom-call(f32[512,512]{1,0:T(8,128)S(1)} %get-tuple-element.10.factor_in, bf16[256,256]{1,0:T(8,128)(2,1)S(1)} %get-tuple-element.11.w1, bf16[256,256]{1,0:T(8,128)(2,1)S(1)} %get-tuple-element.12.w2, bf16[256,256]{1,0:T(8,128)(2,1)S(1)} %get-tuple-element.13.cross, ...), custom_call_target="tpu_custom_call" | custom-call | tf_op jit(solution)/shard_map/rotate/pallas_call | solution.py:609
